TPU v7x, 256 devices: a whole 4x4x8 slice. The times are simulated.
256 devices in a mesh: own: 8 (over y_lo, x), br: 32 (over z, y_hi, core).
Axes of the slice: x: 4, y: 4 (y_hi: 2, y_lo: 2; y = y_hi * 2 + y_lo), z: 8, core: 2. Of those that a mesh axis runs over, the one named last changes fastest.
Arguments:
- queries: bfloat16 [128, 256, 5120], P('br', None, 'own'), may hold values from -6 to 6
- branch_keys: bfloat16 [128, 256, 1024], P('br', None, 'own'), may hold values from -6 to 6
- branch_values: bfloat16 [128, 256, 1024], P('br', None, 'own'), may hold values from -6 to 6
- attn_out: bfloat16 [128, 256, 5120], P('br', None, 'own'), may hold values from -6 to 6
- out_grad: bfloat16 [128, 256, 5120], P('br', None, 'own'), may hold values from -6 to 6
- logsumexp: float32 [128, 40, 256], P('br', 'own'), may hold values from 7 to 8.5
- prefix_keys: bfloat16 [512, 8, 1024], P('br', 'own'), may hold values from -6 to 6
- prefix_values: bfloat16 [512, 8, 1024], P('br', 'own'), may hold values from -6 to 6
- prefix_of: int32 [128], P('br'), may hold values from 0 to 7
- counts: int32 [32], P('br'), may hold values from 1 to 4, as said below
Outputs:
- query_grad: bfloat16 [128, 256, 5120], P('br', None, 'own')
- key_grad: bfloat16 [128, 256, 1024], P('br', None, 'own')
- value_grad: bfloat16 [128, 256, 1024], P('br', None, 'own')
- prefix_key_grad: bfloat16 [512, 8, 1024], P('br', 'own')
- prefix_value_grad: bfloat16 [512, 8, 1024], P('br', 'own')
Inputs may be any that keep to these rules, and one draw needn't show every extreme that they name: The first counts[b] of the 4 slots of br index b hold branches, the other slots are empty; some br index is full in every draw.
All inputs are finite; a program needn't handle non-finite values.
Results may differ from a plain program's by a relative error of at most 0.0049.
Values may be sent and summed in bfloat16 or wider, within the bound.
No kernel may reach another device: no remote copies, remote signals or barrier semaphores. Data moves between devices by JAX's collectives and lax.ppermute only.
A program may use at most 64 MiB of HBM per device.

v0:
```python
import functools

import jax
import jax.numpy as jnp
from jax import lax
from jax.experimental import pallas as pl
from jax.experimental.pallas import tpu as pltpu
from jax.sharding import PartitionSpec as P

QH = 40
KVH = 8
HD = 128
GROUPS = QH // KVH
SCALE = HD ** (-0.5)
NZ, NY, NC = 8, 2, 2
OWN = 8
KERNEL_VMEM = 24 << 20
NZ, NY, NC = 8, 2, 2
OWN = 8
KERNEL_VMEM = 24 << 20
NEAR_WEIGHT = 0.01


def br_index(z, y, c):
    return (z % NZ) * NY * NC + y * NC + c


def ring_perm(hops):
    return [
        (br_index(z, y, c), br_index(z + (hops if c == 0 else -hops), y, c))
        for z in range(NZ)
        for y in range(NY)
        for c in range(NC)
    ]


CORE_SWAP = [(i, i ^ 1) for i in range(NZ * NY * NC)]
PLANES = [
    [br_index(z, y, c) * OWN + o for y in range(NY) for c in range(NC) for o in range(OWN)]
    for z in range(NZ)
]


def plane_exchange(blocks):
    return lax.all_to_all(
        blocks, ("br", "own"), split_axis=0, concat_axis=0, tiled=True, axis_index_groups=PLANES
    )


def dot_nt(a, b):
    return lax.dot_general(a, b, (((1,), (1,)), ((), ())), preferred_element_type=jnp.float32)


def dot_nn(a, b):
    return lax.dot_general(a, b, (((1,), (0,)), ((), ())), preferred_element_type=jnp.float32)


def dot_tn(a, b):
    return lax.dot_general(a, b, (((0,), (0,)), ((), ())), preferred_element_type=jnp.float32)


def heads_of(ref, slot):
    return [ref[slot, :, g * HD : (g + 1) * HD] for g in range(GROUPS)]


def attention_grads(k, v, qs, dos, lses, deltas, visible=None):
    probs = [jnp.exp(dot_nt(k, q) * SCALE - lse) for q, lse in zip(qs, lses)]
    if visible is not None:
        probs = [jnp.where(visible, prob, 0.0) for prob in probs]
    dprobs = [dot_nt(v, do) for do in dos]
    dscores = [
        (prob * (dprob - delta)).astype(jnp.bfloat16)
        for prob, dprob, delta in zip(probs, dprobs, deltas)
    ]
    probs = [prob.astype(jnp.bfloat16) for prob in probs]
    dk = SCALE * dot_nn(jnp.concatenate(dscores, 1), jnp.concatenate(qs, 0))
    dv = dot_nn(jnp.concatenate(probs, 1), jnp.concatenate(dos, 0))
    dqs = [SCALE * dot_tn(dscore, k) for dscore in dscores]
    return dqs, dk, dv


def vmem():
    return pl.BlockSpec(memory_space=pltpu.VMEM)


def smem():
    return pl.BlockSpec(memory_space=pltpu.SMEM)


def send_kernel(key_ref, value_ref, out_ref):
    for h in range(KVH):
        cols = slice(h * HD, (h + 1) * HD)
        key, value = key_ref[:, cols], value_ref[:, cols]
        for block in range(NY * NC):
            out_ref[block * KVH + h, :, :HD] = key
            out_ref[block * KVH + h, :, HD:] = value


def send_part(prefix_keys, prefix_values):
    rows = prefix_keys.shape[0]
    flat = (rows, KVH * HD)
    return pl.pallas_call(
        send_kernel,
        in_specs=[vmem()] * 2,
        out_specs=vmem(),
        out_shape=jax.ShapeDtypeStruct((NY * NC * KVH, rows, 2 * HD), jnp.bfloat16),
        name="send_part",
    )(prefix_keys.reshape(flat), prefix_values.reshape(flat))


def home_kernel(in_ref, key_ref, value_ref):
    for h in range(KVH):
        cols = slice(h * HD, (h + 1) * HD)
        parts = [in_ref[block * KVH + h].astype(jnp.float32) for block in range(NY * NC)]
        total = ((parts[0] + parts[1]) + (parts[2] + parts[3])).astype(jnp.bfloat16)
        key_ref[:, cols] = total[:, :HD]
        value_ref[:, cols] = total[:, HD:]


def home_part(received):
    rows = received.shape[1]
    shape = jax.ShapeDtypeStruct((rows, KVH * HD), jnp.bfloat16)
    grads = pl.pallas_call(
        home_kernel,
        in_specs=[vmem()],
        out_specs=[vmem()] * 2,
        out_shape=[shape, shape],
        name="home_part",
    )(received)
    return [grad.reshape(rows, 1, KVH * HD) for grad in grads]


def self_kernel(
    count_ref, q_ref, k_ref, v_ref, o_ref, do_ref, lse_ref, dq_ref, dk_ref, dv_ref, stat_ref
):
    live = pl.program_id(0) < count_ref[0]

    @pl.when(live)
    def _():
        k, v = k_ref[0], v_ref[0]
        length = k.shape[0]
        row = lax.broadcasted_iota(jnp.int32, (length, length), 0)
        token = lax.broadcasted_iota(jnp.int32, (length, length), 1)
        qs, dos, outs = heads_of(q_ref, 0), heads_of(do_ref, 0), heads_of(o_ref, 0)
        lses = [lse_ref[0, g : g + 1, :] for g in range(GROUPS)]
        deltas = [
            jnp.sum((do.astype(jnp.float32) * o.astype(jnp.float32)).T, axis=0, keepdims=True)
            for do, o in zip(dos, outs)
        ]
        for g in range(GROUPS):
            stat_ref[0, g : g + 1, :] = lses[g]
            stat_ref[0, 8 + g : 9 + g, :] = deltas[g]
        dqs, dk, dv = attention_grads(k, v, qs, dos, lses, deltas, row <= token)
        for g in range(GROUPS):
            dq_ref[0, :, g * HD : (g + 1) * HD] = dqs[g].astype(dq_ref.dtype)
        dk_ref[0] = dk.astype(jnp.bfloat16)
        dv_ref[0] = dv.astype(jnp.bfloat16)

    @pl.when(jnp.logical_not(live))
    def _():
        for ref in (dq_ref, dk_ref, dv_ref, stat_ref):
            ref[...] = jnp.zeros_like(ref)


def self_part(count, queries, keys, values, attn_out, out_grad, logsumexp):
    slots, length, width = queries.shape

    def spec(*shape):
        return pl.BlockSpec((1,) + shape, lambda i: (i, 0, 0))

    wide, narrow = spec(length, width), spec(length, HD)
    return pl.pallas_call(
        self_kernel,
        grid=(slots,),
        in_specs=[smem(), wide, narrow, narrow, wide, wide, spec(GROUPS, length)],
        out_specs=[wide, narrow, narrow, spec(16, length)],
        out_shape=[
            jax.ShapeDtypeStruct((slots, length, width), jnp.bfloat16),
            jax.ShapeDtypeStruct((slots, length, HD), jnp.bfloat16),
            jax.ShapeDtypeStruct((slots, length, HD), jnp.bfloat16),
            jax.ShapeDtypeStruct((slots, 16, length), jnp.float32),
        ],
        compiler_params=pltpu.CompilerParams(vmem_limit_bytes=KERNEL_VMEM),
        cost_estimate=pl.CostEstimate(
            flops=slots * 10 * length * length * width,
            bytes_accessed=slots * length * width * 10,
            transcendentals=slots * length * length * GROUPS,
        ),
        name="self_part",
    )(count, queries, keys, values, attn_out, out_grad, logsumexp)


def prefix_kernel(n_pieces, slots, with_oth, pre_ref, *refs):
    refs = list(refs)
    take = lambda n: [refs.pop(0) for _ in range(n)]
    q_own, do_own, stat_own, q_oth, do_oth, stat_oth, more_own = take(7)
    more_oth = take(1)[0] if with_oth else None
    pieces = take(n_pieces)
    dq_own, dq_oth = take(2)
    outs = take(n_pieces)
    (acc,) = refs
    step = pl.program_id(0)
    prefix = pre_ref[step]

    @pl.when(step == 0)
    def _():
        acc[...] = jnp.zeros_like(acc)

    def work(q_ref, do_ref, stat_ref, more_ref, dq_ref):
        @pl.when(prefix >= 0)
        def _():
            rows = [p[:, prefix] for p in pieces]
            kv = jnp.concatenate([r.reshape(r.shape[0] * r.shape[1], 2 * HD) for r in rows], 0)
            k, v = kv[:, :HD], kv[:, HD:]
            dqs, dk, dv = attention_grads(
                k,
                v,
                heads_of(q_ref, 0),
                heads_of(do_ref, 0),
                [stat_ref[0, g : g + 1, :] for g in range(GROUPS)],
                [stat_ref[0, 8 + g : 9 + g, :] for g in range(GROUPS)],
            )
            for g in range(GROUPS):
                cols = slice(g * HD, (g + 1) * HD)
                dq = dqs[g]
                if more_ref is not None:
                    dq += more_ref[0, :, cols].astype(jnp.float32)
                dq_ref[0, :, cols] = dq.astype(dq_ref.dtype)
            acc[prefix, :, :HD] += dk
            acc[prefix, :, HD:] += dv

        @pl.when(prefix < 0)
        def _():
            dq_ref[...] = jnp.zeros_like(dq_ref)

    @pl.when(step < slots)
    def _():
        work(q_own, do_own, stat_own, more_own, dq_own)

    @pl.when(step >= slots)
    def _():
        work(q_oth, do_oth, stat_oth, more_oth, dq_oth)

    @pl.when(step == 2 * slots - 1)
    def _():
        start = 0
        for out in outs:
            for block in range(out.shape[0]):
                out[block] = acc[:, start : start + out.shape[2], :].astype(out.dtype)
                start += out.shape[2]


def prefix_part(prefixes, own, oth, pieces, name):
    slots, length, width = own[0].shape
    n_rows = sum(p.shape[0] * p.shape[2] for p in pieces)
    n_pre = pieces[0].shape[1]

    def first(*shape):
        return pl.BlockSpec((1,) + shape, lambda i, c: (jnp.minimum(i, slots - 1), 0, 0))

    def second(*shape):
        return pl.BlockSpec((1,) + shape, lambda i, c: (jnp.maximum(i - slots, 0), 0, 0))

    def whole(p):
        return pl.BlockSpec(p.shape, lambda i, c: (0, 0, 0, 0))

    in_specs = [first(*a.shape[1:]) for a in own[:3]] + [second(*a.shape[1:]) for a in oth[:3]]
    in_specs += [first(length, width)] + [second(length, width) for _ in oth[3:]]
    return pl.pallas_call(
        functools.partial(prefix_kernel, len(pieces), slots, len(oth) > 3),
        grid_spec=pltpu.PrefetchScalarGridSpec(
            num_scalar_prefetch=1,
            grid=(2 * slots,),
            in_specs=in_specs + [whole(p) for p in pieces],
            out_specs=[first(length, width), second(length, width)] + [whole(p) for p in pieces],
            scratch_shapes=[pltpu.VMEM((n_pre, n_rows, 2 * HD), jnp.float32)],
        ),
        out_shape=[
            jax.ShapeDtypeStruct((slots, length, width), jnp.bfloat16),
            jax.ShapeDtypeStruct((slots, length, width), jnp.bfloat16),
        ]
        + [jax.ShapeDtypeStruct(p.shape, jnp.bfloat16) for p in pieces],
        compiler_params=pltpu.CompilerParams(vmem_limit_bytes=KERNEL_VMEM),
        cost_estimate=pl.CostEstimate(
            flops=2 * slots * 10 * length * n_rows * width,
            bytes_accessed=slots * length * width * 16,
            transcendentals=2 * slots * length * n_rows * GROUPS,
        ),
        name=name,
    )(prefixes, *own[:3], *oth[:3], own[3], *oth[3:], *pieces)


def per_device(
    queries,
    branch_keys,
    branch_values,
    attn_out,
    out_grad,
    logsumexp,
    prefix_keys,
    prefix_values,
    prefix_of,
    counts,
):
    slots = queries.shape[0]
    rows, n_pre = prefix_keys.shape[0], OWN
    core = lax.rem(lax.axis_index("br"), NC)
    swap = functools.partial(lax.ppermute, axis_name="br", perm=CORE_SWAP)

    f32, bf16 = jnp.float32, jnp.bfloat16
    plane = plane_exchange(send_part(prefix_keys, prefix_values))
    plane = plane.reshape(NY * NC, n_pre, rows, 2 * HD)

    mine = jnp.where(jnp.arange(slots) < counts[0], prefix_of, -1)
    prefixes = jnp.concatenate([mine, swap(mine)])
    q_oth, do_oth = swap(queries), swap(out_grad)
    plane, prefixes, q_oth, do_oth, count = lax.optimization_barrier(
        (plane, prefixes, q_oth, do_oth, counts)
    )
    own_half = lax.dynamic_slice_in_dim(plane, core * (NY * NC // 2), NY * NC // 2, 0)
    one = lax.ppermute(plane, "br", ring_perm(1))
    two = lax.ppermute(plane, "br", ring_perm(2))
    three = lax.ppermute(one, "br", ring_perm(2))
    two_half = lax.dynamic_slice_in_dim(two, core * (NY * NC // 2), NY * NC // 2, 0)
    four = lax.ppermute(two_half, "br", ring_perm(2))
    dq_self, key_grad, value_grad, stat = self_part(
        count, queries, branch_keys, branch_values, attn_out, out_grad, logsumexp
    )
    stat_oth = swap(stat)
    dq_own, dq_oth, g_own, g1, g2, g3, g4 = prefix_part(
        prefixes,
        (queries, out_grad, stat, dq_self),
        (q_oth, do_oth, stat_oth),
        (own_half, one, two, three, four),
        "prefix_part",
    )
    h4 = lax.ppermute(g4, "br", ring_perm(-4))
    h3 = lax.ppermute(g3, "br", ring_perm(-3))
    h2 = lax.ppermute(g2, "br", ring_perm(-2))
    h1 = lax.ppermute(g1, "br", ring_perm(-1))
    dq_back = swap(dq_oth)
    query_grad = (dq_own.astype(f32) + dq_back.astype(f32)).astype(bf16)

    in_half = (jnp.arange(NY * NC) // (NY * NC // 2) == core)[:, None, None, None]
    halves = g_own.astype(f32) + h4.astype(f32)
    spread = jnp.where(in_half, jnp.concatenate([halves, halves], 0), 0.0)
    near = h1.astype(f32) + h2.astype(f32)
    total = (near + (h3.astype(f32) + spread)).astype(bf16)
    total, query_grad = lax.optimization_barrier((total, query_grad))
    prefix_key_grad, prefix_value_grad = home_part(
        plane_exchange(total.reshape(NY * NC * n_pre, rows, 2 * HD))
    )
    return (query_grad, key_grad, value_grad, prefix_key_grad, prefix_value_grad)


def solution(mesh):
    placed = (
        P("br", None, "own"),
        P("br", None, "own"),
        P("br", None, "own"),
        P("br", None, "own"),
        P("br", None, "own"),
        P("br", "own", None),
        P("br", "own", None),
        P("br", "own", None),
        P("br"),
        P("br"),
    )
    return jax.shard_map(
        per_device,
        mesh=mesh,
        in_specs=placed,
        out_specs=(
            P("br", None, "own"),
            P("br", None, "own"),
            P("br", None, "own"),
            P("br", "own", None),
            P("br", "own", None),
        ),
        check_vma=False,
    )
```

profile of v0, /device:TPU:1, one launch (start us, length us, event | category | flops | bytes accessed | tf_op | source)
XLA Modules:
  0.0 103.0 jit_solution(15485016710441581974)
XLA Ops:
  0.6 3.3 %collective-permute-start.1 = (bf16[4,256,640]{2,1,0:T(8,128)(2,1)}, bf16[4,256,640]{2,1,0:T(8,128)(2,1)S(1)}, u32[]{:S(2)}, u32[]{:S(2)}) collective-permute-start(bf16[4,256,640]{2,1,0:T(8,128)(2,1)} %refs_0_.1), channel_id=1, source_target_pairs={{0,1},{1,0},{2,3},{3,2},{4,5},{5,4},{6,7},{7,6},{8,9},{9,8},{10,11... | collective-permute-start | bytes 3932168 | tf_op jit(solution)/shard_map/ppermute | solution.py:316
  4.0 0.1 collective-permute-start.2
  4.1 1.5 %send_part.1 = bf16[32,16,256]{2,1,0:T(8,128)(2,1)} custom-call(bf16[16,1024]{1,0:T(8,128)(2,1)} %bitcast.12, bf16[16,1024]{1,0:T(8,128)(2,1)} %bitcast.13), custom_call_target="tpu_custom_call" | custom-call | tf_op jit(solution)/shard_map/send_part/pallas_call | solution.py:102
  5.6 5.8 %all-to-all-start = ((bf16[32,16,256]{2,1,0:T(8,128)(2,1)}), bf16[32,16,256]{2,1,0:T(8,128)(2,1)S(1)}, u32[]{:S(2)}, u32[]{:S(2)}) async-start(bf16[32,16,256]{2,1,0:T(8,128)(2,1)} %send_part.1), calls=%async_computation | async-start | bytes 524288 | tf_op jit(solution)/shard_map/all_to_all | solution.py:45
  12.0 0.7 compare_select_fusion
  12.6 0.2 collective-permute-start
  12.9 0.9 collective-permute-done
  13.8 0.1 pad_add_fusion.pre_ref
  13.8 6.2 %all-to-all-done = bf16[32,16,256]{2,1,0:T(8,128)(2,1)S(1)} async-done(((bf16[32,16,256]{2,1,0:T(8,128)(2,1)}), bf16[32,16,256]{2,1,0:T(8,128)(2,1)S(1)}, u32[]{:S(2)}, u32[]{:S(2)}) %all-to-all-start) | async-done | bytes 262176 | tf_op jit(solution)/shard_map/all_to_all | solution.py:45
  20.1 0.0 collective-permute-done.1.refs_3_
  20.1 0.0 collective-permute-done.2.refs_4_
  20.1 6.0 %collective-permute-start.5 = (bf16[4,8,16,256]{3,2,1,0:T(8,128)(2,1)S(1)}, bf16[4,8,16,256]{3,2,1,0:T(8,128)(2,1)S(1)}, u32[]{:S(2)}, u32[]{:S(2)}) collective-permute-start(bf16[4,8,16,256]{3,2,1,0:T(8,128)(2,1)S(1)} %bitcast.9), channel_id=1, source_target_pairs={{0,8},{1,25},{2,10},{3,27},{4,12},{5,29},{6,14},{7,31},{8,16},{9,1... | collective-permute-start | bytes 786440 | tf_op jit(solution)/shard_map/ppermute | solution.py:322
  26.1 0.7 collective-permute-start.4
  26.9 0.7 copy.15.lse_ref
  27.6 4.7 %collective-permute-done.5.refs_9_ = bf16[4,8,16,256]{3,2,1,0:T(8,128)(2,1)S(1)} collective-permute-done((bf16[4,8,16,256]{3,2,1,0:T(8,128)(2,1)S(1)}, bf16[4,8,16,256]{3,2,1,0:T(8,128)(2,1)S(1)}, u32[]{:S(2)}, u32[]{:S(2)}) %collective-permute-start.5) | collective-permute-done | bytes 262176 | tf_op jit(solution)/shard_map/ppermute | solution.py:322
  32.3 4.2 %collective-permute-start.7 = (bf16[2,8,16,256]{3,2,1,0:T(8,128)(2,1)S(1)}, bf16[2,8,16,256]{3,2,1,0:T(8,128)(2,1)S(1)}, u32[]{:S(2)}, u32[]{:S(2)}) collective-permute-start(bf16[2,8,16,256]{3,2,1,0:T(8,128)(2,1)S(1)} %constant_dynamic-slice_fusion), channel_id=1, source_target_pairs={{0,8},{1,25},{2,10},{3,27},{4,12},{5,29},{6,14},{7,31},{8,16},{9,1... | collective-permute-start | bytes 393224 | tf_op jit(solution)/shard_map/ppermute | solution.py:325
  36.5 0.0 collective-permute-done.4.refs_8_
  36.5 1.3 %collective-permute-start.6 = (bf16[4,8,16,256]{3,2,1,0:T(8,128)(2,1)S(1)}, bf16[4,8,16,256]{3,2,1,0:T(8,128)(2,1)S(1)}, u32[]{:S(2)}, u32[]{:S(2)}) collective-permute-start(bf16[4,8,16,256]{3,2,1,0:T(8,128)(2,1)S(1)} %collective-permute-done.4.refs_8_), channel_id=1, source_target_pairs={{0,8},{1,25},{2,10},{3,27},{4,12},{5,29},{6,14},{7,31},{8,16},{9,1... | collective-permute-start | bytes 786440 | tf_op jit(solution)/shard_map/ppermute | solution.py:323
  37.7 0.0 copy-start
  37.8 1.3 %copy-done = bf16[4,256,640]{2,1,0:T(8,128)(2,1)S(1)} copy-done((bf16[4,256,640]{2,1,0:T(8,128)(2,1)S(1)}, bf16[4,256,640]{2,1,0:T(8,128)(2,1)}, u32[]{:S(2)}) %copy-start) | copy-done | bytes 1310744
  39.1 0.0 copy-start.1
  39.1 1.3 %copy-done.1 = bf16[4,256,640]{2,1,0:T(8,128)(2,1)S(1)} copy-done((bf16[4,256,640]{2,1,0:T(8,128)(2,1)S(1)}, bf16[4,256,640]{2,1,0:T(8,128)(2,1)}, u32[]{:S(2)}) %copy-start.1) | copy-done | bytes 1310744
  40.4 0.0 copy-start.2
  40.4 1.3 %copy-done.2 = bf16[4,256,640]{2,1,0:T(8,128)(2,1)S(1)} copy-done((bf16[4,256,640]{2,1,0:T(8,128)(2,1)S(1)}, bf16[4,256,640]{2,1,0:T(8,128)(2,1)}, u32[]{:S(2)}) %copy-start.2) | copy-done | bytes 1310744
  41.7 0.0 copy-start.4
  41.7 0.9 copy-done.4
  42.7 0.9 copy-done.5
  43.6 5.3 %self_part.1 = (bf16[4,256,640]{2,1,0:T(8,128)(2,1)S(1)}, bf16[4,256,128]{2,1,0:T(8,128)(2,1)}, bf16[4,256,128]{2,1,0:T(8,128)(2,1)}, f32[4,16,256]{2,1,0:T(8,128)S(1)}) custom-call(s32[1]{0:T(128)} %copy.16.count_ref, bf16[4,256,640]{2,1,0:T(8,128)(2,1)S(1)} %copy-done.1, bf16[4,256,128]{2,1,0:T(8,128)(2,1)S(1)} %copy-done.4, ...), custom_call_target="tpu_custom_call" | custom-call | flops 1677721600 | bytes 6553600 | tf_op jit(solution)/shard_map/self_part/pallas_call | solution.py:172
  48.9 0.0 collective-permute-start.3
  48.9 1.2 %collective-permute-done.3.refs_5_ = f32[4,16,256]{2,1,0:T(8,128)S(1)} collective-permute-done((f32[4,16,256]{2,1,0:T(8,128)S(1)}, f32[4,16,256]{2,1,0:T(8,128)S(1)}, u32[]{:S(2)}, u32[]{:S(2)}) %collective-permute-start.3) | collective-permute-done | bytes 65568 | tf_op jit(solution)/shard_map/ppermute | solution.py:329
  50.1 0.0 collective-permute-done.7.refs_11_
  50.1 0.0 collective-permute-done.6.refs_10_
  50.1 0.0 copy-done.3
  50.1 6.5 %prefix_part.1 = (bf16[4,256,640]{2,1,0:T(8,128)(2,1)S(1)}, bf16[4,256,640]{2,1,0:T(8,128)(2,1)S(1)}, bf16[2,8,16,256]{3,2,1,0:T(8,128)(2,1)S(1)}, bf16[4,8,16,2...) custom-call(s32[8]{0:T(128)S(1)} %pad_add_fusion.pre_ref, ...), custom_call_target="tpu_custom_call" | custom-call | flops 3355443200 | bytes 10485760 | tf_op jit(solution)/shard_map/prefix_part/pallas_call | solution.py:269
  56.7 0.2 collective-permute-start.12
  56.9 0.0 collective-permute-start.11
  56.9 6.3 %collective-permute-start.8 = (bf16[4,8,16,256]{3,2,1,0:T(8,128)(2,1)S(1)}, bf16[4,8,16,256]{3,2,1,0:T(8,128)(2,1)S(1)}, u32[]{:S(2)}, u32[]{:S(2)}) collective-permute-start(bf16[4,8,16,256]{3,2,1,0:T(8,128)(2,1)S(1)} %get-tuple-element.32), channel_id=1, source_target_pairs={{0,28},{1,5},{2,30},{3,7},{4,0},{5,9},{6,2},{7,11},{8,4},{9,13},{1... | collective-permute-start | bytes 786440 | tf_op jit(solution)/shard_map/ppermute | solution.py:340
  63.2 0.0 collective-permute-start.9
  63.2 5.2 %collective-permute-start.10 = (bf16[4,8,16,256]{3,2,1,0:T(8,128)(2,1)S(1)}, bf16[4,8,16,256]{3,2,1,0:T(8,128)(2,1)S(1)}, u32[]{:S(2)}, u32[]{:S(2)}) collective-permute-start(bf16[4,8,16,256]{3,2,1,0:T(8,128)(2,1)S(1)} %get-tuple-element.34), channel_id=1, source_target_pairs={{0,20},{1,13},{2,22},{3,15},{4,24},{5,17},{6,26},{7,19},{8,28},{9,... | collective-permute-start | bytes 786440 | tf_op jit(solution)/shard_map/ppermute | solution.py:338
  68.4 0.0 collective-permute-done.11
  68.5 0.0 collective-permute-done.8
  68.5 2.2 %collective-permute-done.9 = bf16[4,8,16,256]{3,2,1,0:T(8,128)(2,1)S(1)} collective-permute-done((bf16[4,8,16,256]{3,2,1,0:T(8,128)(2,1)S(1)}, bf16[4,8,16,256]{3,2,1,0:T(8,128)(2,1)S(1)}, u32[]{:S(2)}, u32[]{:S(2)}) %collective-permute-start.9) | collective-permute-done | bytes 262176 | tf_op jit(solution)/shard_map/ppermute | solution.py:339
  70.6 12.9 %collective-permute-done.10 = bf16[4,8,16,256]{3,2,1,0:T(8,128)(2,1)S(1)} collective-permute-done((bf16[4,8,16,256]{3,2,1,0:T(8,128)(2,1)S(1)}, bf16[4,8,16,256]{3,2,1,0:T(8,128)(2,1)S(1)}, u32[]{:S(2)}, u32[]{:S(2)}) %collective-permute-start.10) | collective-permute-done | bytes 262176 | tf_op jit(solution)/shard_map/ppermute | solution.py:338
  83.5 0.2 fusion.2
  83.7 0.0 collective-permute-done.12
  83.7 1.4 %add_convert_fusion = bf16[4,256,640]{2,1,0:T(8,128)(2,1)} fusion(bf16[4,256,640]{2,1,0:T(8,128)(2,1)S(1)} %collective-permute-done.12, bf16[4,256,640]{2,1,0:T(8,128)(2,1)S(1)} %get-tuple-element.37), kind=kLoop, calls=%fused_computation | loop fusion | flops 2621440 | bytes 3932160 | tf_op jit(solution)/shard_map/convert_element_type | solution.py:342
  85.1 16.3 %all_to_all.10.in_ref = bf16[32,16,256]{2,1,0:T(8,128)(2,1)} all-to-all(bf16[32,16,256]{2,1,0:T(8,128)(2,1)S(1)} %bitcast.8), channel_id=1, replica_groups={{0,32,64,96,128,160,192,224,1,33,65,97,129,161,193,225,2,34,66,98,130,1..., dimensions={0} | all-to-all | bytes 524288 | tf_op jit(solution)/shard_map/all_to_all | solution.py:45
  101.4 1.6 %home_part.1 = (bf16[16,1024]{1,0:T(8,128)(2,1)}, bf16[16,1024]{1,0:T(8,128)(2,1)}) custom-call(bf16[32,16,256]{2,1,0:T(8,128)(2,1)} %all_to_all.10.in_ref), custom_call_target="tpu_custom_call" | custom-call | tf_op jit(solution)/shard_map/home_part/pallas_call | solution.py:123
  (6 shorter events, 0.1 us)
Async XLA Ops:
  0.6 19.5 %collective-permute-start.1 = (bf16[4,256,640]{2,1,0:T(8,128)(2,1)}, bf16[4,256,640]{2,1,0:T(8,128)(2,1)S(1)}, u32[]{:S(2)}, u32[]{:S(2)}) collective-permute-start(bf16[4,256,640]{2,1,0:T(8,128)(2,1)} %refs_0_.1), channel_id=1, source_target_pairs={{0,1},{1,0},{2,3},{3,2},{4,5},{5,4},{6,7},{7,6},{8,9},{9,8},{10,11... | collective-permute-start | bytes 3932168 | tf_op jit(solution)/shard_map/ppermute | solution.py:316
  4.0 16.1 %collective-permute-start.2 = (bf16[4,256,640]{2,1,0:T(8,128)(2,1)}, bf16[4,256,640]{2,1,0:T(8,128)(2,1)S(1)}, u32[]{:S(2)}, u32[]{:S(2)}) collective-permute-start(bf16[4,256,640]{2,1,0:T(8,128)(2,1)} %refs_1_.1), channel_id=1, source_target_pairs={{0,1},{1,0},{2,3},{3,2},{4,5},{5,4},{6,7},{7,6},{8,9},{9,8},{10,11... | collective-permute-start | bytes 3932168 | tf_op jit(solution)/shard_map/ppermute | solution.py:316
  5.6 14.5 %all-to-all-start = ((bf16[32,16,256]{2,1,0:T(8,128)(2,1)}), bf16[32,16,256]{2,1,0:T(8,128)(2,1)S(1)}, u32[]{:S(2)}, u32[]{:S(2)}) async-start(bf16[32,16,256]{2,1,0:T(8,128)(2,1)} %send_part.1), calls=%async_computation | async-start | bytes 524288 | tf_op jit(solution)/shard_map/all_to_all | solution.py:45
  12.6 1.1 %collective-permute-start = (s32[4]{0:T(128)S(1)}, s32[4]{0:T(128)S(1)}, u32[]{:S(2)}, u32[]{:S(2)}) collective-permute-start(s32[4]{0:T(128)S(1)} %compare_select_fusion), channel_id=1, source_target_pairs={{0,1},{1,0},{2,3},{3,2},{4,5},{5,4},{6,7},{7,6},{8,9},{9,8},{10,11... | collective-permute-start | bytes 56 | tf_op jit(solution)/shard_map/ppermute | solution.py:315
  20.1 12.1 %collective-permute-start.5 = (bf16[4,8,16,256]{3,2,1,0:T(8,128)(2,1)S(1)}, bf16[4,8,16,256]{3,2,1,0:T(8,128)(2,1)S(1)}, u32[]{:S(2)}, u32[]{:S(2)}) collective-permute-start(bf16[4,8,16,256]{3,2,1,0:T(8,128)(2,1)S(1)} %bitcast.9), channel_id=1, source_target_pairs={{0,8},{1,25},{2,10},{3,27},{4,12},{5,29},{6,14},{7,31},{8,16},{9,1... | collective-permute-start | bytes 786440 | tf_op jit(solution)/shard_map/ppermute | solution.py:322
  26.1 10.3 %collective-permute-start.4 = (bf16[4,8,16,256]{3,2,1,0:T(8,128)(2,1)S(1)}, bf16[4,8,16,256]{3,2,1,0:T(8,128)(2,1)S(1)}, u32[]{:S(2)}, u32[]{:S(2)}) collective-permute-start(bf16[4,8,16,256]{3,2,1,0:T(8,128)(2,1)S(1)} %bitcast.10), channel_id=1, source_target_pairs={{0,4},{1,29},{2,6},{3,31},{4,8},{5,1},{6,10},{7,3},{8,12},{9,5},{1... | collective-permute-start | bytes 786440 | tf_op jit(solution)/shard_map/ppermute | solution.py:321
  32.3 17.9 %collective-permute-start.7 = (bf16[2,8,16,256]{3,2,1,0:T(8,128)(2,1)S(1)}, bf16[2,8,16,256]{3,2,1,0:T(8,128)(2,1)S(1)}, u32[]{:S(2)}, u32[]{:S(2)}) collective-permute-start(bf16[2,8,16,256]{3,2,1,0:T(8,128)(2,1)S(1)} %constant_dynamic-slice_fusion), channel_id=1, source_target_pairs={{0,8},{1,25},{2,10},{3,27},{4,12},{5,29},{6,14},{7,31},{8,16},{9,1... | collective-permute-start | bytes 393224 | tf_op jit(solution)/shard_map/ppermute | solution.py:325
  36.5 13.7 %collective-permute-start.6 = (bf16[4,8,16,256]{3,2,1,0:T(8,128)(2,1)S(1)}, bf16[4,8,16,256]{3,2,1,0:T(8,128)(2,1)S(1)}, u32[]{:S(2)}, u32[]{:S(2)}) collective-permute-start(bf16[4,8,16,256]{3,2,1,0:T(8,128)(2,1)S(1)} %collective-permute-done.4.refs_8_), channel_id=1, source_target_pairs={{0,8},{1,25},{2,10},{3,27},{4,12},{5,29},{6,14},{7,31},{8,16},{9,1... | collective-permute-start | bytes 786440 | tf_op jit(solution)/shard_map/ppermute | solution.py:323
  37.7 1.3 %copy-start = (bf16[4,256,640]{2,1,0:T(8,128)(2,1)S(1)}, bf16[4,256,640]{2,1,0:T(8,128)(2,1)}, u32[]{:S(2)}) copy-start(bf16[4,256,640]{2,1,0:T(8,128)(2,1)} %o_ref.1) | copy-start | bytes 3932164
  39.1 1.3 %copy-start.1 = (bf16[4,256,640]{2,1,0:T(8,128)(2,1)S(1)}, bf16[4,256,640]{2,1,0:T(8,128)(2,1)}, u32[]{:S(2)}) copy-start(bf16[4,256,640]{2,1,0:T(8,128)(2,1)} %refs_0_.1) | copy-start | bytes 3932164
  40.4 1.3 %copy-start.2 = (bf16[4,256,640]{2,1,0:T(8,128)(2,1)S(1)}, bf16[4,256,640]{2,1,0:T(8,128)(2,1)}, u32[]{:S(2)}) copy-start(bf16[4,256,640]{2,1,0:T(8,128)(2,1)} %refs_1_.1) | copy-start | bytes 3932164
  41.7 0.9 copy-start.4
  42.7 0.9 copy-start.5
  43.6 6.5 %copy-start.3 = (bf16[4,256,640]{2,1,0:T(8,128)(2,1)S(1)}, bf16[4,256,640]{2,1,0:T(8,128)(2,1)}, u32[]{:S(2)}) copy-start(bf16[4,256,640]{2,1,0:T(8,128)(2,1)} %refs_1_.1) | copy-start | bytes 3932164
  48.9 1.3 %collective-permute-start.3 = (f32[4,16,256]{2,1,0:T(8,128)S(1)}, f32[4,16,256]{2,1,0:T(8,128)S(1)}, u32[]{:S(2)}, u32[]{:S(2)}) collective-permute-start(f32[4,16,256]{2,1,0:T(8,128)S(1)} %get-tuple-element.27.refs_2_), channel_id=1, source_target_pairs={{0,1},{1,0},{2,3},{3,2},{4,5},{5,4},{6,7},{7,6},{8,9},{9,8},{10,11... | collective-permute-start | bytes 196616 | tf_op jit(solution)/shard_map/ppermute | solution.py:329
  56.7 27.0 %collective-permute-start.12 = (bf16[4,256,640]{2,1,0:T(8,128)(2,1)S(1)}, bf16[4,256,640]{2,1,0:T(8,128)(2,1)S(1)}, u32[]{:S(2)}, u32[]{:S(2)}) collective-permute-start(bf16[4,256,640]{2,1,0:T(8,128)(2,1)S(1)} %get-tuple-element.38), channel_id=1, source_target_pairs={{0,1},{1,0},{2,3},{3,2},{4,5},{5,4},{6,7},{7,6},{8,9},{9,8},{10,11... | collective-permute-start | bytes 3932168 | tf_op jit(solution)/shard_map/ppermute | solution.py:341
  56.9 11.5 %collective-permute-start.11 = (bf16[2,8,16,256]{3,2,1,0:T(8,128)(2,1)S(1)}, bf16[2,8,16,256]{3,2,1,0:T(8,128)(2,1)S(1)}, u32[]{:S(2)}, u32[]{:S(2)}) collective-permute-start(bf16[2,8,16,256]{3,2,1,0:T(8,128)(2,1)S(1)} %get-tuple-element.36), channel_id=1, source_target_pairs={{0,16},{1,17},{2,18},{3,19},{4,20},{5,21},{6,22},{7,23},{8,24},{9,... | collective-permute-start | bytes 393224 | tf_op jit(solution)/shard_map/ppermute | solution.py:337
  56.9 11.6 %collective-permute-start.8 = (bf16[4,8,16,256]{3,2,1,0:T(8,128)(2,1)S(1)}, bf16[4,8,16,256]{3,2,1,0:T(8,128)(2,1)S(1)}, u32[]{:S(2)}, u32[]{:S(2)}) collective-permute-start(bf16[4,8,16,256]{3,2,1,0:T(8,128)(2,1)S(1)} %get-tuple-element.32), channel_id=1, source_target_pairs={{0,28},{1,5},{2,30},{3,7},{4,0},{5,9},{6,2},{7,11},{8,4},{9,13},{1... | collective-permute-start | bytes 786440 | tf_op jit(solution)/shard_map/ppermute | solution.py:340
  63.2 7.4 %collective-permute-start.9 = (bf16[4,8,16,256]{3,2,1,0:T(8,128)(2,1)S(1)}, bf16[4,8,16,256]{3,2,1,0:T(8,128)(2,1)S(1)}, u32[]{:S(2)}, u32[]{:S(2)}) collective-permute-start(bf16[4,8,16,256]{3,2,1,0:T(8,128)(2,1)S(1)} %get-tuple-element.33), channel_id=1, source_target_pairs={{0,24},{1,9},{2,26},{3,11},{4,28},{5,13},{6,30},{7,15},{8,0},{9,17... | collective-permute-start | bytes 786440 | tf_op jit(solution)/shard_map/ppermute | solution.py:339
  63.2 20.3 %collective-permute-start.10 = (bf16[4,8,16,256]{3,2,1,0:T(8,128)(2,1)S(1)}, bf16[4,8,16,256]{3,2,1,0:T(8,128)(2,1)S(1)}, u32[]{:S(2)}, u32[]{:S(2)}) collective-permute-start(bf16[4,8,16,256]{3,2,1,0:T(8,128)(2,1)S(1)} %get-tuple-element.34), channel_id=1, source_target_pairs={{0,20},{1,13},{2,22},{3,15},{4,24},{5,17},{6,26},{7,19},{8,28},{9,... | collective-permute-start | bytes 786440 | tf_op jit(solution)/shard_map/ppermute | solution.py:338
where the time goes:
time: 102 us; the launch traced here: 103 us
  starting transfers between devices  33.4 us (33%)
  waiting for transfers between devices  28.1 us (28%)
  blocking collectives  16.3 us (16%)
  Pallas kernels  14.9 us (15%)
  local copies, waits for them, and re-layouts  6.6 us (6%)
  other arithmetic  2.32 us (2%)
  between operations  1.36 us (1%)
    all_to_all x1, blocking collectives, plane_exchange(): lax.all_to_all(blocks, ('br', 'own'), split_axis=0, concat_axis=0, tiled=...  16.3 us
    ppermute x1, waiting for transfers between devices, per_device(): h3 = lax.ppermute(g3, 'br', ring_perm(-3))  12.9 us
    unnamed x13, local copies, waits for them, and re-layouts  6.58 us
    pallas_call x1, Pallas kernels, prefix_part(): pl.pallas_call(functools.partial(prefix_kernel, len(pieces), slots, len(o...  6.53 us
    ppermute x1, starting transfers between devices, per_device(): h1 = lax.ppermute(g1, 'br', ring_perm(-1))  6.31 us
    all_to_all x1, waiting for transfers between devices, plane_exchange(): lax.all_to_all(blocks, ('br', 'own'), split_axis=0, concat_axis=0, tiled=...  6.25 us
    ppermute x1, starting transfers between devices, per_device(): two = lax.ppermute(plane, 'br', ring_perm(2))  6.02 us
    all_to_all x1, starting transfers between devices, plane_exchange(): lax.all_to_all(blocks, ('br', 'own'), split_axis=0, concat_axis=0, tiled=...  5.76 us
  transfers between devices with their start and end apart: 14, of which 6 were waited for; matrix products, arithmetic and copies ran while one was open for 2% of the time, Pallas kernels for 7%

commit v1 on v0

--- a/solution.py
+++ b/solution.py
@@ -130,9 +130,36 @@
     return [grad.reshape(rows, 1, KVH * HD) for grad in grads]
 
 
-def self_kernel(
-    count_ref, q_ref, k_ref, v_ref, o_ref, do_ref, lse_ref, dq_ref, dk_ref, dv_ref, stat_ref
-):
+def slot_spec(*shape):
+    return pl.BlockSpec((1,) + shape, lambda i: (i, 0, 0))
+
+
+def stat_kernel(o_ref, do_ref, lse_ref, stat_ref):
+    stat_ref[0, :GROUPS, :] = lse_ref[0]
+    for g, (do, o) in enumerate(zip(heads_of(do_ref, 0), heads_of(o_ref, 0))):
+        product = do.astype(jnp.float32) * o.astype(jnp.float32)
+        stat_ref[0, 8 + g : 9 + g, :] = jnp.sum(product.T, axis=0, keepdims=True)
+
+
+def stat_part(attn_out, out_grad, logsumexp):
+    slots, length, width = attn_out.shape
+    return pl.pallas_call(
+        stat_kernel,
+        grid=(slots,),
+        in_specs=[slot_spec(length, width), slot_spec(length, width), slot_spec(GROUPS, length)],
+        out_specs=slot_spec(16, length),
+        out_shape=jax.ShapeDtypeStruct((slots, 16, length), jnp.float32),
+        compiler_params=pltpu.CompilerParams(vmem_limit_bytes=KERNEL_VMEM),
+        cost_estimate=pl.CostEstimate(
+            flops=slots * 2 * length * width,
+            bytes_accessed=slots * length * width * 4,
+            transcendentals=0,
+        ),
+        name="stat_part",
+    )(attn_out, out_grad, logsumexp)
+
+
+def self_kernel(count_ref, q_ref, k_ref, v_ref, do_ref, stat_ref, dq_ref, dk_ref, dv_ref):
     live = pl.program_id(0) < count_ref[0]
 
     @pl.when(live)
@@ -141,16 +168,15 @@
         length = k.shape[0]
         row = lax.broadcasted_iota(jnp.int32, (length, length), 0)
         token = lax.broadcasted_iota(jnp.int32, (length, length), 1)
-        qs, dos, outs = heads_of(q_ref, 0), heads_of(do_ref, 0), heads_of(o_ref, 0)
-        lses = [lse_ref[0, g : g + 1, :] for g in range(GROUPS)]
-        deltas = [
-            jnp.sum((do.astype(jnp.float32) * o.astype(jnp.float32)).T, axis=0, keepdims=True)
-            for do, o in zip(dos, outs)
-        ]
-        for g in range(GROUPS):
-            stat_ref[0, g : g + 1, :] = lses[g]
-            stat_ref[0, 8 + g : 9 + g, :] = deltas[g]
-        dqs, dk, dv = attention_grads(k, v, qs, dos, lses, deltas, row <= token)
+        dqs, dk, dv = attention_grads(
+            k,
+            v,
+            heads_of(q_ref, 0),
+            heads_of(do_ref, 0),
+            [stat_ref[0, g : g + 1, :] for g in range(GROUPS)],
+            [stat_ref[0, 8 + g : 9 + g, :] for g in range(GROUPS)],
+            row <= token,
+        )
         for g in range(GROUPS):
             dq_ref[0, :, g * HD : (g + 1) * HD] = dqs[g].astype(dq_ref.dtype)
         dk_ref[0] = dk.astype(jnp.bfloat16)
@@ -158,27 +184,22 @@
 
     @pl.when(jnp.logical_not(live))
     def _():
-        for ref in (dq_ref, dk_ref, dv_ref, stat_ref):
+        for ref in (dq_ref, dk_ref, dv_ref):
             ref[...] = jnp.zeros_like(ref)
 
 
-def self_part(count, queries, keys, values, attn_out, out_grad, logsumexp):
+def self_part(count, queries, keys, values, out_grad, stat):
     slots, length, width = queries.shape
-
-    def spec(*shape):
-        return pl.BlockSpec((1,) + shape, lambda i: (i, 0, 0))
-
-    wide, narrow = spec(length, width), spec(length, HD)
+    wide, narrow = slot_spec(length, width), slot_spec(length, HD)
     return pl.pallas_call(
         self_kernel,
         grid=(slots,),
-        in_specs=[smem(), wide, narrow, narrow, wide, wide, spec(GROUPS, length)],
-        out_specs=[wide, narrow, narrow, spec(16, length)],
+        in_specs=[smem(), wide, narrow, narrow, wide, slot_spec(16, length)],
+        out_specs=[wide, narrow, narrow],
         out_shape=[
             jax.ShapeDtypeStruct((slots, length, width), jnp.bfloat16),
             jax.ShapeDtypeStruct((slots, length, HD), jnp.bfloat16),
             jax.ShapeDtypeStruct((slots, length, HD), jnp.bfloat16),
-            jax.ShapeDtypeStruct((slots, 16, length), jnp.float32),
         ],
         compiler_params=pltpu.CompilerParams(vmem_limit_bytes=KERNEL_VMEM),
         cost_estimate=pl.CostEstimate(
@@ -187,7 +208,7 @@
             transcendentals=slots * length * length * GROUPS,
         ),
         name="self_part",
-    )(count, queries, keys, values, attn_out, out_grad, logsumexp)
+    )(count, queries, keys, values, out_grad, stat)
 
 
 def prefix_kernel(n_pieces, slots, with_oth, pre_ref, *refs):
@@ -314,19 +335,20 @@
     mine = jnp.where(jnp.arange(slots) < counts[0], prefix_of, -1)
     prefixes = jnp.concatenate([mine, swap(mine)])
     q_oth, do_oth = swap(queries), swap(out_grad)
-    plane, prefixes, q_oth, do_oth, count = lax.optimization_barrier(
-        (plane, prefixes, q_oth, do_oth, counts)
+    stat = stat_part(attn_out, out_grad, logsumexp)
+    stat_oth = swap(stat)
+    plane, prefixes, q_oth, do_oth, count, stat, stat_oth = lax.optimization_barrier(
+        (plane, prefixes, q_oth, do_oth, counts, stat, stat_oth)
     )
     own_half = lax.dynamic_slice_in_dim(plane, core * (NY * NC // 2), NY * NC // 2, 0)
     one = lax.ppermute(plane, "br", ring_perm(1))
     two = lax.ppermute(plane, "br", ring_perm(2))
-    three = lax.ppermute(one, "br", ring_perm(2))
-    two_half = lax.dynamic_slice_in_dim(two, core * (NY * NC // 2), NY * NC // 2, 0)
-    four = lax.ppermute(two_half, "br", ring_perm(2))
-    dq_self, key_grad, value_grad, stat = self_part(
-        count, queries, branch_keys, branch_values, attn_out, out_grad, logsumexp
-    )
-    stat_oth = swap(stat)
+    three = lax.ppermute(plane, "br", ring_perm(3))
+    half_three = lax.dynamic_slice_in_dim(three, core * (NY * NC // 2), NY * NC // 2, 0)
+    four = lax.ppermute(half_three, "br", ring_perm(1))
+    dq_self, key_grad, value_grad = self_part(
+        count, queries, branch_keys, branch_values, out_grad, stat
+    )
     dq_own, dq_oth, g_own, g1, g2, g3, g4 = prefix_part(
         prefixes,
         (queries, out_grad, stat, dq_self),
@@ -334,19 +356,19 @@
         (own_half, one, two, three, four),
         "prefix_part",
     )
-    h4 = lax.ppermute(g4, "br", ring_perm(-4))
-    h3 = lax.ppermute(g3, "br", ring_perm(-3))
+    in_half = (jnp.arange(NY * NC) // (NY * NC // 2) == core)[:, None, None, None]
+    far = lax.ppermute(g4, "br", ring_perm(-1)).astype(f32)
+    far = jnp.where(in_half, jnp.concatenate([far, far], 0), 0.0)
+    h3 = lax.ppermute((g3.astype(f32) + far).astype(bf16), "br", ring_perm(-3))
     h2 = lax.ppermute(g2, "br", ring_perm(-2))
     h1 = lax.ppermute(g1, "br", ring_perm(-1))
     dq_back = swap(dq_oth)
     query_grad = (dq_own.astype(f32) + dq_back.astype(f32)).astype(bf16)
 
-    in_half = (jnp.arange(NY * NC) // (NY * NC // 2) == core)[:, None, None, None]
-    halves = g_own.astype(f32) + h4.astype(f32)
+    near, query_grad = lax.optimization_barrier((h1.astype(f32) + h2.astype(f32), query_grad))
+    halves = g_own.astype(f32)
     spread = jnp.where(in_half, jnp.concatenate([halves, halves], 0), 0.0)
-    near = h1.astype(f32) + h2.astype(f32)
     total = (near + (h3.astype(f32) + spread)).astype(bf16)
-    total, query_grad = lax.optimization_barrier((total, query_grad))
     prefix_key_grad, prefix_value_grad = home_part(
         plane_exchange(total.reshape(NY * NC * n_pre, rows, 2 * HD))
     )

time: 102 us -> 94.3 us (0.925); the launches traced: 103 us -> 94.3 us
  starting transfers between devices: 33.4 us -> 19.4 us
  waiting for transfers between devices: 28.1 us -> 33.6 us
  Pallas kernels: 14.9 us -> 19.9 us
  blocking collectives: 16.3 us -> 13.4 us
  local copies, waits for them, and re-layouts: 6.6 us -> 4.1 us
    ppermute x4, waiting for transfers between devices: 12.9 us -> 21.1 us  [the longest x1 10.8 us: per_device(): three = lax.ppermute(plane, 'br', ring_perm(3))]
    ppermute x1, starting transfers between devices: 6.31 us -> 0.01 us  [per_device(): h1 = lax.ppermute(g1, 'br', ring_perm(-1))]
    ppermute x1, starting transfers between devices: 6.02 us -> 0.27 us  [per_device(): two = lax.ppermute(plane, 'br', ring_perm(2))]
    all_to_all x1, waiting for transfers between devices: 6.25 us -> 1.48 us  [plane_exchange(): lax.all_to_all(blocks, ('br', 'own'), split_axis=0, concat_axis=0, tiled=...]
    ppermute x1, waiting for transfers between devices: 4.66 us -> 0.01 us  [per_device(): two = lax.ppermute(plane, 'br', ring_perm(2))]
    ppermute x1, waiting for transfers between devices: 2.15 us -> 6.64 us  [per_device(): h2 = lax.ppermute(g2, 'br', ring_perm(-2))]
    pallas_call x1, Pallas kernels: 6.53 us -> 10.8 us  [prefix_part(): pl.pallas_call(functools.partial(prefix_kernel, len(pieces), slots, len(o...]
    ppermute x4, starting transfers between devices: 10.7 us -> 6.71 us  [the longest x1 6.46 us: per_device(): three = lax.ppermute(plane, 'br', ring_perm(3))]
  transfers between devices with their start and end apart: 14 -> 14, of which waited for: 6 -> 9; matrix products, arithmetic and copies ran while one was open for 2% -> 3% of each run, Pallas kernels for 7% -> 8%
where the time goes in v1:
time: 94.3 us
  waiting for transfers between devices  33.6 us (36%)
  Pallas kernels  19.9 us (21%)
  starting transfers between devices  19.4 us (21%)
  blocking collectives  13.4 us (14%)
  local copies, waits for them, and re-layouts  4.1 us (4%)
  other arithmetic  2.57 us (3%)
  between operations  1.39 us (1%)
    all_to_all x1, blocking collectives, plane_exchange(): lax.all_to_all(blocks, ('br', 'own'), split_axis=0, concat_axis=0, tiled=...  13.4 us
    ppermute x1, waiting for transfers between devices, per_device(): three = lax.ppermute(plane, 'br', ring_perm(3))  10.8 us
    pallas_call x1, Pallas kernels, prefix_part(): pl.pallas_call(functools.partial(prefix_kernel, len(pieces), slots, len(o...  10.8 us
    ppermute x1, waiting for transfers between devices, per_device(): h2 = lax.ppermute(g2, 'br', ring_perm(-2))  6.64 us
    ppermute x1, starting transfers between devices, per_device(): three = lax.ppermute(plane, 'br', ring_perm(3))  6.46 us
    all_to_all x1, starting transfers between devices, plane_exchange(): lax.all_to_all(blocks, ('br', 'own'), split_axis=0, concat_axis=0, tiled=...  5.89 us
    pallas_call x1, Pallas kernels, self_part(): pl.pallas_call(self_kernel, grid=(slots,), in_specs=[smem(), wide, narrow...  5 us
    ppermute x1, waiting for transfers between devices, per_device(): h3 = lax.ppermute((g3.astype(f32) + far).astype(bf16), 'br', ring_perm(-3))  4.91 us
  transfers between devices with their start and end apart: 14, of which 9 were waited for; matrix products, arithmetic and copies ran while one was open for 3% of the time, Pallas kernels for 8%

profile of v1, /device:TPU:1, one launch (start us, length us, event | category | flops | bytes accessed | tf_op | source)
XLA Modules:
  0.0 94.3 jit_solution(11752747078514216745)
XLA Ops:
  0.6 3.3 %collective-permute-start.1 = (bf16[4,256,640]{2,1,0:T(8,128)(2,1)}, bf16[4,256,640]{2,1,0:T(8,128)(2,1)}, u32[]{:S(2)}, u32[]{:S(2)}) collective-permute-start(bf16[4,256,640]{2,1,0:T(8,128)(2,1)} %refs_0_.1), channel_id=1, source_target_pairs={{0,1},{1,0},{2,3},{3,2},{4,5},{5,4},{6,7},{7,6},{8,9},{9,8},{10,11... | collective-permute-start | bytes 3932168 | tf_op jit(solution)/shard_map/ppermute | solution.py:337
  4.0 0.1 collective-permute-start.2
  4.1 1.5 %send_part.1 = bf16[32,16,256]{2,1,0:T(8,128)(2,1)} custom-call(bf16[16,1024]{1,0:T(8,128)(2,1)} %bitcast.13, bf16[16,1024]{1,0:T(8,128)(2,1)} %bitcast.14), custom_call_target="tpu_custom_call" | custom-call | tf_op jit(solution)/shard_map/send_part/pallas_call | solution.py:102
  5.6 5.9 %all-to-all-start = ((bf16[32,16,256]{2,1,0:T(8,128)(2,1)}), bf16[32,16,256]{2,1,0:T(8,128)(2,1)S(1)}, u32[]{:S(2)}, u32[]{:S(2)}) async-start(bf16[32,16,256]{2,1,0:T(8,128)(2,1)} %send_part.1), calls=%async_computation | async-start | bytes 524288 | tf_op jit(solution)/shard_map/all_to_all | solution.py:45
  12.1 0.7 compare_select_fusion
  12.8 0.2 collective-permute-start
  13.0 0.7 copy.15.lse_ref
  13.8 1.3 %copy-done = bf16[4,256,640]{2,1,0:T(8,128)(2,1)S(1)} copy-done((bf16[4,256,640]{2,1,0:T(8,128)(2,1)S(1)}, bf16[4,256,640]{2,1,0:T(8,128)(2,1)}, u32[]{:S(2)}) %copy-start) | copy-done | bytes 1310744
  15.1 1.3 %copy-done.1 = bf16[4,256,640]{2,1,0:T(8,128)(2,1)S(1)} copy-done((bf16[4,256,640]{2,1,0:T(8,128)(2,1)S(1)}, bf16[4,256,640]{2,1,0:T(8,128)(2,1)}, u32[]{:S(2)}) %copy-start.1) | copy-done | bytes 1310744
  16.4 1.0 %stat_part.1.stat_ref.refs_2_ = f32[4,16,256]{2,1,0:T(8,128)S(1)} custom-call(bf16[4,256,640]{2,1,0:T(8,128)(2,1)S(1)} %copy-done, bf16[4,256,640]{2,1,0:T(8,128)(2,1)S(1)} %copy-done.1, f32[4,5,256]{2,1,0:T(8,128)S(1)} %copy.15.lse_ref), custom_call_target="tpu_custom_call" | custom-call | flops 1310720 | bytes 2621440 | tf_op jit(solution)/shard_map/stat_part/pallas_call | solution.py:146
  17.4 0.4 collective-permute-start.3
  17.8 0.0 collective-permute-done
  17.8 0.1 pad_add_fusion.pre_ref
  17.9 0.9 collective-permute-done.3.refs_5_
  18.8 1.5 %all-to-all-done = bf16[32,16,256]{2,1,0:T(8,128)(2,1)S(1)} async-done(((bf16[32,16,256]{2,1,0:T(8,128)(2,1)}), bf16[32,16,256]{2,1,0:T(8,128)(2,1)S(1)}, u32[]{:S(2)}, u32[]{:S(2)}) %all-to-all-start) | async-done | bytes 262176 | tf_op jit(solution)/shard_map/all_to_all | solution.py:45
  20.2 0.0 collective-permute-done.1.refs_3_
  20.2 0.0 collective-permute-done.2.refs_4_
  20.2 0.7 copy-done.6
  20.9 6.5 %collective-permute-start.6 = (bf16[4,8,16,256]{3,2,1,0:T(8,128)(2,1)}, bf16[4,8,16,256]{3,2,1,0:T(8,128)(2,1)S(1)}, u32[]{:S(2)}, u32[]{:S(2)}) collective-permute-start(bf16[4,8,16,256]{3,2,1,0:T(8,128)(2,1)} %bitcast.9), channel_id=1, source_target_pairs={{0,12},{1,21},{2,14},{3,23},{4,16},{5,25},{6,18},{7,27},{8,20},{9,... | collective-permute-start | bytes 786440 | tf_op jit(solution)/shard_map/ppermute | solution.py:346
  27.4 0.3 collective-permute-start.5
  27.7 0.5 collective-permute-start.4
  28.1 10.8 %collective-permute-done.6.refs_10_ = bf16[4,8,16,256]{3,2,1,0:T(8,128)(2,1)S(1)} collective-permute-done((bf16[4,8,16,256]{3,2,1,0:T(8,128)(2,1)}, bf16[4,8,16,256]{3,2,1,0:T(8,128)(2,1)S(1)}, u32[]{:S(2)}, u32[]{:S(2)}) %collective-permute-start.6) | collective-permute-done | bytes 262176 | tf_op jit(solution)/shard_map/ppermute | solution.py:346
  39.0 0.0 copy-start.7
  39.0 0.2 collective-permute-start.7
  39.2 0.0 copy-done.5
  39.2 0.0 copy-done.2
  39.2 0.0 copy-done.3
  39.2 5.0 %self_part.1 = (bf16[4,256,640]{2,1,0:T(8,128)(2,1)S(1)}, bf16[4,256,128]{2,1,0:T(8,128)(2,1)}, bf16[4,256,128]{2,1,0:T(8,128)(2,1)}) custom-call(s32[1]{0:T(128)} %copy.16.count_ref, bf16[4,256,640]{2,1,0:T(8,128)(2,1)S(1)} %copy-done.3, bf16[4,256,128]{2,1,0:T(8,128)(2,1)S(1)} %copy-done.4, bf16[4,256,128]{2,1,0:T(8,128)(2,1)S(1)} %copy-done.5, ...), custom_call_target="tpu_custom_call" | custom-call | flops 1677721600 | bytes 6553600 | tf_op jit(solution)/shard_map/self_part/pallas_call | solution.py:194
  44.2 0.0 collective-permute-done.5.refs_9_
  44.2 0.9 collective-permute-done.4.refs_8_
  45.1 1.3 %collective-permute-done.7.refs_11_ = bf16[2,8,16,256]{3,2,1,0:T(8,128)(2,1)S(1)} collective-permute-done((bf16[2,8,16,256]{3,2,1,0:T(8,128)(2,1)S(1)}, bf16[2,8,16,256]{3,2,1,0:T(8,128)(2,1)S(1)}, u32[]{:S(2)}, u32[]{:S(2)}) %collective-permute-start.7) | collective-permute-done | bytes 131104 | tf_op jit(solution)/shard_map/ppermute | solution.py:348
  46.4 10.8 %prefix_part.1 = (bf16[4,256,640]{2,1,0:T(8,128)(2,1)S(1)}, bf16[4,256,640]{2,1,0:T(8,128)(2,1)S(1)}, bf16[2,8,16,256]{3,2,1,0:T(8,128)(2,1)S(1)}, bf16[4,8,16,2...) custom-call(s32[8]{0:T(128)S(1)} %pad_add_fusion.pre_ref, ...), custom_call_target="tpu_custom_call" | custom-call | flops 3355443200 | bytes 10485760 | tf_op jit(solution)/shard_map/prefix_part/pallas_call | solution.py:290
  57.1 1.0 %collective-permute-start.10 = (bf16[4,256,640]{2,1,0:T(8,128)(2,1)S(1)}, bf16[4,256,640]{2,1,0:T(8,128)(2,1)S(1)}, u32[]{:S(2)}, u32[]{:S(2)}) collective-permute-start(bf16[4,256,640]{2,1,0:T(8,128)(2,1)S(1)} %get-tuple-element.37), channel_id=1, source_target_pairs={{0,1},{1,0},{2,3},{3,2},{4,5},{5,4},{6,7},{7,6},{8,9},{9,8},{10,11... | collective-permute-start | bytes 3932168 | tf_op jit(solution)/shard_map/ppermute | solution.py:365
  58.2 0.0 collective-permute-start.11
  58.2 0.0 collective-permute-start.8
  58.2 0.9 %collective-permute-start.9 = (bf16[4,8,16,256]{3,2,1,0:T(8,128)(2,1)S(1)}, bf16[4,8,16,256]{3,2,1,0:T(8,128)(2,1)S(1)}, u32[]{:S(2)}, u32[]{:S(2)}) collective-permute-start(bf16[4,8,16,256]{3,2,1,0:T(8,128)(2,1)S(1)} %get-tuple-element.35), channel_id=1, source_target_pairs={{0,24},{1,9},{2,26},{3,11},{4,28},{5,13},{6,30},{7,15},{8,0},{9,17... | collective-permute-start | bytes 786440 | tf_op jit(solution)/shard_map/ppermute | solution.py:363
  59.1 4.1 %collective-permute-done.11 = bf16[2,8,16,256]{3,2,1,0:T(8,128)(2,1)S(1)} collective-permute-done((bf16[2,8,16,256]{3,2,1,0:T(8,128)(2,1)S(1)}, bf16[2,8,16,256]{3,2,1,0:T(8,128)(2,1)S(1)}, u32[]{:S(2)}, u32[]{:S(2)}) %collective-permute-start.11) | collective-permute-done | bytes 131104 | tf_op jit(solution)/shard_map/ppermute | solution.py:360
  63.2 0.2 add_convert_fusion.2
  63.4 0.1 collective-permute-start.12
  63.5 2.5 %collective-permute-done.8 = bf16[4,8,16,256]{3,2,1,0:T(8,128)(2,1)S(1)} collective-permute-done((bf16[4,8,16,256]{3,2,1,0:T(8,128)(2,1)S(1)}, bf16[4,8,16,256]{3,2,1,0:T(8,128)(2,1)S(1)}, u32[]{:S(2)}, u32[]{:S(2)}) %collective-permute-start.8) | collective-permute-done | bytes 262176 | tf_op jit(solution)/shard_map/ppermute | solution.py:364
  66.0 6.6 %collective-permute-done.9 = bf16[4,8,16,256]{3,2,1,0:T(8,128)(2,1)S(1)} collective-permute-done((bf16[4,8,16,256]{3,2,1,0:T(8,128)(2,1)S(1)}, bf16[4,8,16,256]{3,2,1,0:T(8,128)(2,1)S(1)}, u32[]{:S(2)}, u32[]{:S(2)}) %collective-permute-start.9) | collective-permute-done | bytes 262176 | tf_op jit(solution)/shard_map/ppermute | solution.py:363
  72.7 0.1 convert_add_fusion
  72.7 0.0 collective-permute-done.10
  72.7 1.4 %add_convert_fusion = bf16[4,256,640]{2,1,0:T(8,128)(2,1)} fusion(bf16[4,256,640]{2,1,0:T(8,128)(2,1)S(1)} %collective-permute-done.10, bf16[4,256,640]{2,1,0:T(8,128)(2,1)S(1)} %get-tuple-element.36), kind=kLoop, calls=%fused_computation | loop fusion | flops 2621440 | bytes 3932160 | tf_op jit(solution)/shard_map/convert_element_type | solution.py:366
  74.1 4.9 %collective-permute-done.12 = bf16[4,8,16,256]{3,2,1,0:T(8,128)(2,1)S(1)} collective-permute-done((bf16[4,8,16,256]{3,2,1,0:T(8,128)(2,1)S(1)}, bf16[4,8,16,256]{3,2,1,0:T(8,128)(2,1)S(1)}, u32[]{:S(2)}, u32[]{:S(2)}) %collective-permute-start.12) | collective-permute-done | bytes 262176 | tf_op jit(solution)/shard_map/ppermute | solution.py:362
  79.0 0.2 add_convert_fusion.1
  79.2 13.4 %all_to_all.10.in_ref = bf16[32,16,256]{2,1,0:T(8,128)(2,1)} all-to-all(bf16[32,16,256]{2,1,0:T(8,128)(2,1)S(1)} %bitcast.8), channel_id=1, replica_groups={{0,32,64,96,128,160,192,224,1,33,65,97,129,161,193,225,2,34,66,98,130,1..., dimensions={0} | all-to-all | bytes 524288 | tf_op jit(solution)/shard_map/all_to_all | solution.py:45
  92.7 1.6 %home_part.1 = (bf16[16,1024]{1,0:T(8,128)(2,1)}, bf16[16,1024]{1,0:T(8,128)(2,1)}) custom-call(bf16[32,16,256]{2,1,0:T(8,128)(2,1)} %all_to_all.10.in_ref), custom_call_target="tpu_custom_call" | custom-call | tf_op jit(solution)/shard_map/home_part/pallas_call | solution.py:123
  (12 shorter events, 0.0 us)
Async XLA Ops:
  0.6 19.6 %collective-permute-start.1 = (bf16[4,256,640]{2,1,0:T(8,128)(2,1)}, bf16[4,256,640]{2,1,0:T(8,128)(2,1)}, u32[]{:S(2)}, u32[]{:S(2)}) collective-permute-start(bf16[4,256,640]{2,1,0:T(8,128)(2,1)} %refs_0_.1), channel_id=1, source_target_pairs={{0,1},{1,0},{2,3},{3,2},{4,5},{5,4},{6,7},{7,6},{8,9},{9,8},{10,11... | collective-permute-start | bytes 3932168 | tf_op jit(solution)/shard_map/ppermute | solution.py:337
  4.0 16.3 %collective-permute-start.2 = (bf16[4,256,640]{2,1,0:T(8,128)(2,1)}, bf16[4,256,640]{2,1,0:T(8,128)(2,1)}, u32[]{:S(2)}, u32[]{:S(2)}) collective-permute-start(bf16[4,256,640]{2,1,0:T(8,128)(2,1)} %refs_1_.1), channel_id=1, source_target_pairs={{0,1},{1,0},{2,3},{3,2},{4,5},{5,4},{6,7},{7,6},{8,9},{9,8},{10,11... | collective-permute-start | bytes 3932168 | tf_op jit(solution)/shard_map/ppermute | solution.py:337
  5.6 33.6 %copy-start.5 = (bf16[4,256,128]{2,1,0:T(8,128)(2,1)S(1)}, bf16[4,256,128]{2,1,0:T(8,128)(2,1)}, u32[]{:S(2)}) copy-start(bf16[4,256,128]{2,1,0:T(8,128)(2,1)} %v_ref.1) | copy-start | bytes 786436
  5.6 14.7 %all-to-all-start = ((bf16[32,16,256]{2,1,0:T(8,128)(2,1)}), bf16[32,16,256]{2,1,0:T(8,128)(2,1)S(1)}, u32[]{:S(2)}, u32[]{:S(2)}) async-start(bf16[32,16,256]{2,1,0:T(8,128)(2,1)} %send_part.1), calls=%async_computation | async-start | bytes 524288 | tf_op jit(solution)/shard_map/all_to_all | solution.py:45
  12.8 5.0 %collective-permute-start = (s32[4]{0:T(128)S(1)}, s32[4]{0:T(128)S(1)}, u32[]{:S(2)}, u32[]{:S(2)}) collective-permute-start(s32[4]{0:T(128)S(1)} %compare_select_fusion), channel_id=1, source_target_pairs={{0,1},{1,0},{2,3},{3,2},{4,5},{5,4},{6,7},{7,6},{8,9},{9,8},{10,11... | collective-permute-start | bytes 56 | tf_op jit(solution)/shard_map/ppermute | solution.py:336
  13.7 1.3 %copy-start = (bf16[4,256,640]{2,1,0:T(8,128)(2,1)S(1)}, bf16[4,256,640]{2,1,0:T(8,128)(2,1)}, u32[]{:S(2)}) copy-start(bf16[4,256,640]{2,1,0:T(8,128)(2,1)} %o_ref.1) | copy-start | bytes 3932164
  15.1 1.3 %copy-start.1 = (bf16[4,256,640]{2,1,0:T(8,128)(2,1)S(1)}, bf16[4,256,640]{2,1,0:T(8,128)(2,1)}, u32[]{:S(2)}) copy-start(bf16[4,256,640]{2,1,0:T(8,128)(2,1)} %refs_1_.1) | copy-start | bytes 3932164
  16.4 22.8 %copy-start.2 = (bf16[4,256,640]{2,1,0:T(8,128)(2,1)S(1)}, bf16[4,256,640]{2,1,0:T(8,128)(2,1)}, u32[]{:S(2)}) copy-start(bf16[4,256,640]{2,1,0:T(8,128)(2,1)} %refs_1_.1) | copy-start | bytes 3932164
  16.4 22.8 %copy-start.3 = (bf16[4,256,640]{2,1,0:T(8,128)(2,1)S(1)}, bf16[4,256,640]{2,1,0:T(8,128)(2,1)}, u32[]{:S(2)}) copy-start(bf16[4,256,640]{2,1,0:T(8,128)(2,1)} %refs_0_.1) | copy-start | bytes 3932164
  16.4 22.8 %copy-start.4 = (bf16[4,256,128]{2,1,0:T(8,128)(2,1)S(1)}, bf16[4,256,128]{2,1,0:T(8,128)(2,1)}, u32[]{:S(2)}) copy-start(bf16[4,256,128]{2,1,0:T(8,128)(2,1)} %k_ref.1) | copy-start | bytes 786436
  17.4 1.3 %collective-permute-start.3 = (f32[4,16,256]{2,1,0:T(8,128)S(1)}, f32[4,16,256]{2,1,0:T(8,128)S(1)}, u32[]{:S(2)}, u32[]{:S(2)}) collective-permute-start(f32[4,16,256]{2,1,0:T(8,128)S(1)} %stat_part.1.stat_ref.refs_2_), channel_id=1, source_target_pairs={{0,1},{1,0},{2,3},{3,2},{4,5},{5,4},{6,7},{7,6},{8,9},{9,8},{10,11... | collective-permute-start | bytes 196616 | tf_op jit(solution)/shard_map/ppermute | solution.py:339
  20.2 0.7 copy-start.6
  20.9 18.0 %collective-permute-start.6 = (bf16[4,8,16,256]{3,2,1,0:T(8,128)(2,1)}, bf16[4,8,16,256]{3,2,1,0:T(8,128)(2,1)S(1)}, u32[]{:S(2)}, u32[]{:S(2)}) collective-permute-start(bf16[4,8,16,256]{3,2,1,0:T(8,128)(2,1)} %bitcast.9), channel_id=1, source_target_pairs={{0,12},{1,21},{2,14},{3,23},{4,16},{5,25},{6,18},{7,27},{8,20},{9,... | collective-permute-start | bytes 786440 | tf_op jit(solution)/shard_map/ppermute | solution.py:346
  27.4 16.8 %collective-permute-start.5 = (bf16[4,8,16,256]{3,2,1,0:T(8,128)(2,1)}, bf16[4,8,16,256]{3,2,1,0:T(8,128)(2,1)S(1)}, u32[]{:S(2)}, u32[]{:S(2)}) collective-permute-start(bf16[4,8,16,256]{3,2,1,0:T(8,128)(2,1)} %bitcast.10), channel_id=1, source_target_pairs={{0,8},{1,25},{2,10},{3,27},{4,12},{5,29},{6,14},{7,31},{8,16},{9,1... | collective-permute-start | bytes 786440 | tf_op jit(solution)/shard_map/ppermute | solution.py:345
  27.7 17.4 %collective-permute-start.4 = (bf16[4,8,16,256]{3,2,1,0:T(8,128)(2,1)}, bf16[4,8,16,256]{3,2,1,0:T(8,128)(2,1)S(1)}, u32[]{:S(2)}, u32[]{:S(2)}) collective-permute-start(bf16[4,8,16,256]{3,2,1,0:T(8,128)(2,1)} %bitcast.11), channel_id=1, source_target_pairs={{0,4},{1,29},{2,6},{3,31},{4,8},{5,1},{6,10},{7,3},{8,12},{9,5},{1... | collective-permute-start | bytes 786440 | tf_op jit(solution)/shard_map/ppermute | solution.py:344
  39.0 5.2 %copy-start.7 = (bf16[32,16,256]{2,1,0:T(8,128)(2,1)S(1)}, bf16[32,16,256]{2,1,0:T(8,128)(2,1)}, u32[]{:S(2)}) copy-start(bf16[32,16,256]{2,1,0:T(8,128)(2,1)} %copy-done.6) | copy-start | bytes 786436
  39.0 7.4 %collective-permute-start.7 = (bf16[2,8,16,256]{3,2,1,0:T(8,128)(2,1)S(1)}, bf16[2,8,16,256]{3,2,1,0:T(8,128)(2,1)S(1)}, u32[]{:S(2)}, u32[]{:S(2)}) collective-permute-start(bf16[2,8,16,256]{3,2,1,0:T(8,128)(2,1)S(1)} %constant_dynamic-slice_fusion), channel_id=1, source_target_pairs={{0,4},{1,29},{2,6},{3,31},{4,8},{5,1},{6,10},{7,3},{8,12},{9,5},{1... | collective-permute-start | bytes 393224 | tf_op jit(solution)/shard_map/ppermute | solution.py:348
  57.1 15.6 %collective-permute-start.10 = (bf16[4,256,640]{2,1,0:T(8,128)(2,1)S(1)}, bf16[4,256,640]{2,1,0:T(8,128)(2,1)S(1)}, u32[]{:S(2)}, u32[]{:S(2)}) collective-permute-start(bf16[4,256,640]{2,1,0:T(8,128)(2,1)S(1)} %get-tuple-element.37), channel_id=1, source_target_pairs={{0,1},{1,0},{2,3},{3,2},{4,5},{5,4},{6,7},{7,6},{8,9},{9,8},{10,11... | collective-permute-start | bytes 3932168 | tf_op jit(solution)/shard_map/ppermute | solution.py:365
  58.2 5.0 %collective-permute-start.11 = (bf16[2,8,16,256]{3,2,1,0:T(8,128)(2,1)S(1)}, bf16[2,8,16,256]{3,2,1,0:T(8,128)(2,1)S(1)}, u32[]{:S(2)}, u32[]{:S(2)}) collective-permute-start(bf16[2,8,16,256]{3,2,1,0:T(8,128)(2,1)S(1)} %get-tuple-element.43), channel_id=1, source_target_pairs={{0,28},{1,5},{2,30},{3,7},{4,0},{5,9},{6,2},{7,11},{8,4},{9,13},{1... | collective-permute-start | bytes 393224 | tf_op jit(solution)/shard_map/ppermute | solution.py:360
  58.2 7.8 %collective-permute-start.8 = (bf16[4,8,16,256]{3,2,1,0:T(8,128)(2,1)S(1)}, bf16[4,8,16,256]{3,2,1,0:T(8,128)(2,1)S(1)}, u32[]{:S(2)}, u32[]{:S(2)}) collective-permute-start(bf16[4,8,16,256]{3,2,1,0:T(8,128)(2,1)S(1)} %get-tuple-element.34), channel_id=1, source_target_pairs={{0,28},{1,5},{2,30},{3,7},{4,0},{5,9},{6,2},{7,11},{8,4},{9,13},{1... | collective-permute-start | bytes 786440 | tf_op jit(solution)/shard_map/ppermute | solution.py:364
  58.2 14.5 %collective-permute-start.9 = (bf16[4,8,16,256]{3,2,1,0:T(8,128)(2,1)S(1)}, bf16[4,8,16,256]{3,2,1,0:T(8,128)(2,1)S(1)}, u32[]{:S(2)}, u32[]{:S(2)}) collective-permute-start(bf16[4,8,16,256]{3,2,1,0:T(8,128)(2,1)S(1)} %get-tuple-element.35), channel_id=1, source_target_pairs={{0,24},{1,9},{2,26},{3,11},{4,28},{5,13},{6,30},{7,15},{8,0},{9,17... | collective-permute-start | bytes 786440 | tf_op jit(solution)/shard_map/ppermute | solution.py:363
  63.4 15.7 %collective-permute-start.12 = (bf16[4,8,16,256]{3,2,1,0:T(8,128)(2,1)S(1)}, bf16[4,8,16,256]{3,2,1,0:T(8,128)(2,1)S(1)}, u32[]{:S(2)}, u32[]{:S(2)}) collective-permute-start(bf16[4,8,16,256]{3,2,1,0:T(8,128)(2,1)S(1)} %add_convert_fusion.2), channel_id=1, source_target_pairs={{0,20},{1,13},{2,22},{3,15},{4,24},{5,17},{6,26},{7,19},{8,28},{9,... | collective-permute-start | bytes 786440 | tf_op jit(solution)/shard_map/ppermute | solution.py:362

commit v2 on v1

--- a/solution.py
+++ b/solution.py
@@ -12,6 +12,7 @@
 HD = 128
 GROUPS = QH // KVH
 SCALE = HD ** (-0.5)
+LOG2E = 1.4426950408889634
 NZ, NY, NC = 8, 2, 2
 OWN = 8
 KERNEL_VMEM = 24 << 20
@@ -64,7 +65,7 @@
 
 
 def attention_grads(k, v, qs, dos, lses, deltas, visible=None):
-    probs = [jnp.exp(dot_nt(k, q) * SCALE - lse) for q, lse in zip(qs, lses)]
+    probs = [jnp.exp2(dot_nt(k, q) * (SCALE * LOG2E) - lse * LOG2E) for q, lse in zip(qs, lses)]
     if visible is not None:
         probs = [jnp.where(visible, prob, 0.0) for prob in probs]
     dprobs = [dot_nt(v, do) for do in dos]

time: 94.3 us -> 94.9 us (level)
  Pallas kernels: 19.9 us -> 12.2 us
  starting transfers between devices: 19.4 us -> 25.9 us
  blocking collectives: 13.4 us -> 14.4 us
    ppermute x1, waiting for transfers between devices: 4.91 us -> 10.3 us  [per_device(): h3 = lax.ppermute((g3.astype(f32) + far).astype(bf16), 'br', ring_perm(-3))]
    pallas_call x1, Pallas kernels: 10.8 us -> 5.6 us  [prefix_part(): pl.pallas_call(functools.partial(prefix_kernel, len(pieces), slots, len(o...]
    ppermute x1, waiting for transfers between devices: 4.06 us -> 0.87 us  [per_device(): far = lax.ppermute(g4, 'br', ring_perm(-1)).astype(f32)]
    ppermute x1, starting transfers between devices: 0.94 us -> 3.67 us  [per_device(): h2 = lax.ppermute(g2, 'br', ring_perm(-2))]
    pallas_call x1, Pallas kernels: 5 us -> 2.51 us  [self_part(): pl.pallas_call(self_kernel, grid=(slots,), in_specs=[smem(), wide, narrow...]
    ppermute x1, waiting for transfers between devices: 6.64 us -> 4.32 us  [per_device(): h2 = lax.ppermute(g2, 'br', ring_perm(-2))]
    ppermute x1, waiting for transfers between devices: 0.89 us -> 2.81 us  [per_device(): one = lax.ppermute(plane, 'br', ring_perm(1))]
    ppermute x1, starting transfers between devices: 0.08 us -> 1.91 us  [per_device(): h3 = lax.ppermute((g3.astype(f32) + far).astype(bf16), 'br', ring_perm(-3))]
  transfers between devices with their start and end apart: 14 -> 14, of which waited for: 9 -> 10; matrix products, arithmetic and copies ran while one was open for 3% -> 3% of each run, Pallas kernels for 8% -> 5%
where the time goes in v2:
time: 94.9 us; the launch traced here: 94.7 us
  waiting for transfers between devices  34.1 us (36%)
  starting transfers between devices  25.9 us (27%)
  blocking collectives  14.4 us (15%)
  Pallas kernels  12.2 us (13%)
  local copies, waits for them, and re-layouts  4.1 us (4%)
  other arithmetic  2.57 us (3%)
  between operations  1.37 us (1%)
    all_to_all x1, blocking collectives, plane_exchange(): lax.all_to_all(blocks, ('br', 'own'), split_axis=0, concat_axis=0, tiled=...  14.4 us
    ppermute x1, waiting for transfers between devices, per_device(): three = lax.ppermute(plane, 'br', ring_perm(3))  10.8 us
    ppermute x1, waiting for transfers between devices, per_device(): h3 = lax.ppermute((g3.astype(f32) + far).astype(bf16), 'br', ring_perm(-3))  10.3 us
    ppermute x1, starting transfers between devices, per_device(): three = lax.ppermute(plane, 'br', ring_perm(3))  6.46 us
    all_to_all x1, starting transfers between devices, plane_exchange(): lax.all_to_all(blocks, ('br', 'own'), split_axis=0, concat_axis=0, tiled=...  5.89 us
    pallas_call x1, Pallas kernels, prefix_part(): pl.pallas_call(functools.partial(prefix_kernel, len(pieces), slots, len(o...  5.6 us
    ppermute x1, waiting for transfers between devices, per_device(): h2 = lax.ppermute(g2, 'br', ring_perm(-2))  4.32 us
    unnamed x17, local copies, waits for them, and re-layouts  4.08 us
  transfers between devices with their start and end apart: 14, of which 10 were waited for; matrix products, arithmetic and copies ran while one was open for 3% of the time, Pallas kernels for 5%

profile of v2, /device:TPU:1, one launch (start us, length us, event | category | flops | bytes accessed | tf_op | source)
XLA Modules:
  0.0 94.7 jit_solution(7292443985295910696)
XLA Ops:
  0.6 3.3 %collective-permute-start.1 = (bf16[4,256,640]{2,1,0:T(8,128)(2,1)}, bf16[4,256,640]{2,1,0:T(8,128)(2,1)}, u32[]{:S(2)}, u32[]{:S(2)}) collective-permute-start(bf16[4,256,640]{2,1,0:T(8,128)(2,1)} %refs_0_.1), channel_id=1, source_target_pairs={{0,1},{1,0},{2,3},{3,2},{4,5},{5,4},{6,7},{7,6},{8,9},{9,8},{10,11... | collective-permute-start | bytes 3932168 | tf_op jit(solution)/shard_map/ppermute | solution.py:338
  4.0 0.1 collective-permute-start.2
  4.1 1.5 %send_part.1 = bf16[32,16,256]{2,1,0:T(8,128)(2,1)} custom-call(bf16[16,1024]{1,0:T(8,128)(2,1)} %bitcast.13, bf16[16,1024]{1,0:T(8,128)(2,1)} %bitcast.14), custom_call_target="tpu_custom_call" | custom-call | tf_op jit(solution)/shard_map/send_part/pallas_call | solution.py:103
  5.6 5.9 %all-to-all-start = ((bf16[32,16,256]{2,1,0:T(8,128)(2,1)}), bf16[32,16,256]{2,1,0:T(8,128)(2,1)S(1)}, u32[]{:S(2)}, u32[]{:S(2)}) async-start(bf16[32,16,256]{2,1,0:T(8,128)(2,1)} %send_part.1), calls=%async_computation | async-start | bytes 524288 | tf_op jit(solution)/shard_map/all_to_all | solution.py:46
  12.1 0.7 compare_select_fusion
  12.8 0.2 collective-permute-start
  13.0 0.7 copy.15.lse_ref
  13.8 1.3 %copy-done = bf16[4,256,640]{2,1,0:T(8,128)(2,1)S(1)} copy-done((bf16[4,256,640]{2,1,0:T(8,128)(2,1)S(1)}, bf16[4,256,640]{2,1,0:T(8,128)(2,1)}, u32[]{:S(2)}) %copy-start) | copy-done | bytes 1310744
  15.1 1.3 %copy-done.1 = bf16[4,256,640]{2,1,0:T(8,128)(2,1)S(1)} copy-done((bf16[4,256,640]{2,1,0:T(8,128)(2,1)S(1)}, bf16[4,256,640]{2,1,0:T(8,128)(2,1)}, u32[]{:S(2)}) %copy-start.1) | copy-done | bytes 1310744
  16.4 1.0 %stat_part.1.stat_ref.refs_2_ = f32[4,16,256]{2,1,0:T(8,128)S(1)} custom-call(bf16[4,256,640]{2,1,0:T(8,128)(2,1)S(1)} %copy-done, bf16[4,256,640]{2,1,0:T(8,128)(2,1)S(1)} %copy-done.1, f32[4,5,256]{2,1,0:T(8,128)S(1)} %copy.15.lse_ref), custom_call_target="tpu_custom_call" | custom-call | flops 1310720 | bytes 2621440 | tf_op jit(solution)/shard_map/stat_part/pallas_call | solution.py:147
  17.4 0.4 collective-permute-start.3
  17.8 0.0 collective-permute-done
  17.8 0.1 pad_add_fusion.pre_ref
  17.9 0.9 collective-permute-done.3.refs_5_
  18.8 1.5 %all-to-all-done = bf16[32,16,256]{2,1,0:T(8,128)(2,1)S(1)} async-done(((bf16[32,16,256]{2,1,0:T(8,128)(2,1)}), bf16[32,16,256]{2,1,0:T(8,128)(2,1)S(1)}, u32[]{:S(2)}, u32[]{:S(2)}) %all-to-all-start) | async-done | bytes 262176 | tf_op jit(solution)/shard_map/all_to_all | solution.py:46
  20.2 0.0 collective-permute-done.1.refs_3_
  20.2 0.0 collective-permute-done.2.refs_4_
  20.2 0.7 copy-done.6
  20.9 6.5 %collective-permute-start.6 = (bf16[4,8,16,256]{3,2,1,0:T(8,128)(2,1)}, bf16[4,8,16,256]{3,2,1,0:T(8,128)(2,1)S(1)}, u32[]{:S(2)}, u32[]{:S(2)}) collective-permute-start(bf16[4,8,16,256]{3,2,1,0:T(8,128)(2,1)} %bitcast.9), channel_id=1, source_target_pairs={{0,12},{1,21},{2,14},{3,23},{4,16},{5,25},{6,18},{7,27},{8,20},{9,... | collective-permute-start | bytes 786440 | tf_op jit(solution)/shard_map/ppermute | solution.py:347
  27.4 0.3 collective-permute-start.5
  27.7 0.5 collective-permute-start.4
  28.1 10.8 %collective-permute-done.6.refs_10_ = bf16[4,8,16,256]{3,2,1,0:T(8,128)(2,1)S(1)} collective-permute-done((bf16[4,8,16,256]{3,2,1,0:T(8,128)(2,1)}, bf16[4,8,16,256]{3,2,1,0:T(8,128)(2,1)S(1)}, u32[]{:S(2)}, u32[]{:S(2)}) %collective-permute-start.6) | collective-permute-done | bytes 262176 | tf_op jit(solution)/shard_map/ppermute | solution.py:347
  39.0 0.0 copy-start.7
  39.0 0.2 collective-permute-start.7
  39.2 0.0 copy-done.5
  39.2 0.0 copy-done.2
  39.2 0.0 copy-done.3
  39.2 2.5 %self_part.1 = (bf16[4,256,640]{2,1,0:T(8,128)(2,1)S(1)}, bf16[4,256,128]{2,1,0:T(8,128)(2,1)}, bf16[4,256,128]{2,1,0:T(8,128)(2,1)}) custom-call(s32[1]{0:T(128)} %copy.16.count_ref, bf16[4,256,640]{2,1,0:T(8,128)(2,1)S(1)} %copy-done.3, bf16[4,256,128]{2,1,0:T(8,128)(2,1)S(1)} %copy-done.4, bf16[4,256,128]{2,1,0:T(8,128)(2,1)S(1)} %copy-done.5, ...), custom_call_target="tpu_custom_call" | custom-call | flops 1677721600 | bytes 6553600 | tf_op jit(solution)/shard_map/self_part/pallas_call | solution.py:195
  41.7 0.6 collective-permute-done.5.refs_9_
  42.3 2.8 %collective-permute-done.4.refs_8_ = bf16[4,8,16,256]{3,2,1,0:T(8,128)(2,1)S(1)} collective-permute-done((bf16[4,8,16,256]{3,2,1,0:T(8,128)(2,1)}, bf16[4,8,16,256]{3,2,1,0:T(8,128)(2,1)S(1)}, u32[]{:S(2)}, u32[]{:S(2)}) %collective-permute-start.4) | collective-permute-done | bytes 262176 | tf_op jit(solution)/shard_map/ppermute | solution.py:345
  45.1 1.3 %collective-permute-done.7.refs_11_ = bf16[2,8,16,256]{3,2,1,0:T(8,128)(2,1)S(1)} collective-permute-done((bf16[2,8,16,256]{3,2,1,0:T(8,128)(2,1)S(1)}, bf16[2,8,16,256]{3,2,1,0:T(8,128)(2,1)S(1)}, u32[]{:S(2)}, u32[]{:S(2)}) %collective-permute-start.7) | collective-permute-done | bytes 131104 | tf_op jit(solution)/shard_map/ppermute | solution.py:349
  46.4 5.6 %prefix_part.1 = (bf16[4,256,640]{2,1,0:T(8,128)(2,1)S(1)}, bf16[4,256,640]{2,1,0:T(8,128)(2,1)S(1)}, bf16[2,8,16,256]{3,2,1,0:T(8,128)(2,1)S(1)}, bf16[4,8,16,2...) custom-call(s32[8]{0:T(128)S(1)} %pad_add_fusion.pre_ref, ...), custom_call_target="tpu_custom_call" | custom-call | flops 3355443200 | bytes 10485760 | tf_op jit(solution)/shard_map/prefix_part/pallas_call | solution.py:291
  52.0 1.0 %collective-permute-start.10 = (bf16[4,256,640]{2,1,0:T(8,128)(2,1)S(1)}, bf16[4,256,640]{2,1,0:T(8,128)(2,1)S(1)}, u32[]{:S(2)}, u32[]{:S(2)}) collective-permute-start(bf16[4,256,640]{2,1,0:T(8,128)(2,1)S(1)} %get-tuple-element.37), channel_id=1, source_target_pairs={{0,1},{1,0},{2,3},{3,2},{4,5},{5,4},{6,7},{7,6},{8,9},{9,8},{10,11... | collective-permute-start | bytes 3932168 | tf_op jit(solution)/shard_map/ppermute | solution.py:366
  53.0 0.5 collective-permute-start.11
  53.5 1.6 %collective-permute-start.8 = (bf16[4,8,16,256]{3,2,1,0:T(8,128)(2,1)S(1)}, bf16[4,8,16,256]{3,2,1,0:T(8,128)(2,1)S(1)}, u32[]{:S(2)}, u32[]{:S(2)}) collective-permute-start(bf16[4,8,16,256]{3,2,1,0:T(8,128)(2,1)S(1)} %get-tuple-element.34), channel_id=1, source_target_pairs={{0,28},{1,5},{2,30},{3,7},{4,0},{5,9},{6,2},{7,11},{8,4},{9,13},{1... | collective-permute-start | bytes 786440 | tf_op jit(solution)/shard_map/ppermute | solution.py:365
  55.0 3.7 %collective-permute-start.9 = (bf16[4,8,16,256]{3,2,1,0:T(8,128)(2,1)S(1)}, bf16[4,8,16,256]{3,2,1,0:T(8,128)(2,1)S(1)}, u32[]{:S(2)}, u32[]{:S(2)}) collective-permute-start(bf16[4,8,16,256]{3,2,1,0:T(8,128)(2,1)S(1)} %get-tuple-element.35), channel_id=1, source_target_pairs={{0,24},{1,9},{2,26},{3,11},{4,28},{5,13},{6,30},{7,15},{8,0},{9,17... | collective-permute-start | bytes 786440 | tf_op jit(solution)/shard_map/ppermute | solution.py:364
  58.7 0.9 collective-permute-done.11
  59.6 0.2 add_convert_fusion.2
  59.8 1.9 %collective-permute-start.12 = (bf16[4,8,16,256]{3,2,1,0:T(8,128)(2,1)S(1)}, bf16[4,8,16,256]{3,2,1,0:T(8,128)(2,1)S(1)}, u32[]{:S(2)}, u32[]{:S(2)}) collective-permute-start(bf16[4,8,16,256]{3,2,1,0:T(8,128)(2,1)S(1)} %add_convert_fusion.2), channel_id=1, source_target_pairs={{0,20},{1,13},{2,22},{3,15},{4,24},{5,17},{6,26},{7,19},{8,28},{9,... | collective-permute-start | bytes 786440 | tf_op jit(solution)/shard_map/ppermute | solution.py:363
  61.7 0.7 collective-permute-done.8
  62.4 4.3 %collective-permute-done.9 = bf16[4,8,16,256]{3,2,1,0:T(8,128)(2,1)S(1)} collective-permute-done((bf16[4,8,16,256]{3,2,1,0:T(8,128)(2,1)S(1)}, bf16[4,8,16,256]{3,2,1,0:T(8,128)(2,1)S(1)}, u32[]{:S(2)}, u32[]{:S(2)}) %collective-permute-start.9) | collective-permute-done | bytes 262176 | tf_op jit(solution)/shard_map/ppermute | solution.py:364
  66.7 0.1 convert_add_fusion
  66.8 0.0 collective-permute-done.10
  66.8 1.4 %add_convert_fusion = bf16[4,256,640]{2,1,0:T(8,128)(2,1)} fusion(bf16[4,256,640]{2,1,0:T(8,128)(2,1)S(1)} %collective-permute-done.10, bf16[4,256,640]{2,1,0:T(8,128)(2,1)S(1)} %get-tuple-element.36), kind=kLoop, calls=%fused_computation | loop fusion | flops 2621440 | bytes 3932160 | tf_op jit(solution)/shard_map/convert_element_type | solution.py:367
  68.2 10.3 %collective-permute-done.12 = bf16[4,8,16,256]{3,2,1,0:T(8,128)(2,1)S(1)} collective-permute-done((bf16[4,8,16,256]{3,2,1,0:T(8,128)(2,1)S(1)}, bf16[4,8,16,256]{3,2,1,0:T(8,128)(2,1)S(1)}, u32[]{:S(2)}, u32[]{:S(2)}) %collective-permute-start.12) | collective-permute-done | bytes 262176 | tf_op jit(solution)/shard_map/ppermute | solution.py:363
  78.5 0.2 add_convert_fusion.1
  78.7 14.4 %all_to_all.10.in_ref = bf16[32,16,256]{2,1,0:T(8,128)(2,1)} all-to-all(bf16[32,16,256]{2,1,0:T(8,128)(2,1)S(1)} %bitcast.8), channel_id=1, replica_groups={{0,32,64,96,128,160,192,224,1,33,65,97,129,161,193,225,2,34,66,98,130,1..., dimensions={0} | all-to-all | bytes 524288 | tf_op jit(solution)/shard_map/all_to_all | solution.py:46
  93.1 1.6 %home_part.1 = (bf16[16,1024]{1,0:T(8,128)(2,1)}, bf16[16,1024]{1,0:T(8,128)(2,1)}) custom-call(bf16[32,16,256]{2,1,0:T(8,128)(2,1)} %all_to_all.10.in_ref), custom_call_target="tpu_custom_call" | custom-call | tf_op jit(solution)/shard_map/home_part/pallas_call | solution.py:124
  (12 shorter events, 0.0 us)
Async XLA Ops:
  0.6 19.6 %collective-permute-start.1 = (bf16[4,256,640]{2,1,0:T(8,128)(2,1)}, bf16[4,256,640]{2,1,0:T(8,128)(2,1)}, u32[]{:S(2)}, u32[]{:S(2)}) collective-permute-start(bf16[4,256,640]{2,1,0:T(8,128)(2,1)} %refs_0_.1), channel_id=1, source_target_pairs={{0,1},{1,0},{2,3},{3,2},{4,5},{5,4},{6,7},{7,6},{8,9},{9,8},{10,11... | collective-permute-start | bytes 3932168 | tf_op jit(solution)/shard_map/ppermute | solution.py:338
  4.0 16.3 %collective-permute-start.2 = (bf16[4,256,640]{2,1,0:T(8,128)(2,1)}, bf16[4,256,640]{2,1,0:T(8,128)(2,1)}, u32[]{:S(2)}, u32[]{:S(2)}) collective-permute-start(bf16[4,256,640]{2,1,0:T(8,128)(2,1)} %refs_1_.1), channel_id=1, source_target_pairs={{0,1},{1,0},{2,3},{3,2},{4,5},{5,4},{6,7},{7,6},{8,9},{9,8},{10,11... | collective-permute-start | bytes 3932168 | tf_op jit(solution)/shard_map/ppermute | solution.py:338
  5.6 33.6 %copy-start.5 = (bf16[4,256,128]{2,1,0:T(8,128)(2,1)S(1)}, bf16[4,256,128]{2,1,0:T(8,128)(2,1)}, u32[]{:S(2)}) copy-start(bf16[4,256,128]{2,1,0:T(8,128)(2,1)} %v_ref.1) | copy-start | bytes 786436
  5.6 14.7 %all-to-all-start = ((bf16[32,16,256]{2,1,0:T(8,128)(2,1)}), bf16[32,16,256]{2,1,0:T(8,128)(2,1)S(1)}, u32[]{:S(2)}, u32[]{:S(2)}) async-start(bf16[32,16,256]{2,1,0:T(8,128)(2,1)} %send_part.1), calls=%async_computation | async-start | bytes 524288 | tf_op jit(solution)/shard_map/all_to_all | solution.py:46
  12.8 5.0 %collective-permute-start = (s32[4]{0:T(128)S(1)}, s32[4]{0:T(128)S(1)}, u32[]{:S(2)}, u32[]{:S(2)}) collective-permute-start(s32[4]{0:T(128)S(1)} %compare_select_fusion), channel_id=1, source_target_pairs={{0,1},{1,0},{2,3},{3,2},{4,5},{5,4},{6,7},{7,6},{8,9},{9,8},{10,11... | collective-permute-start | bytes 56 | tf_op jit(solution)/shard_map/ppermute | solution.py:337
  13.7 1.3 %copy-start = (bf16[4,256,640]{2,1,0:T(8,128)(2,1)S(1)}, bf16[4,256,640]{2,1,0:T(8,128)(2,1)}, u32[]{:S(2)}) copy-start(bf16[4,256,640]{2,1,0:T(8,128)(2,1)} %o_ref.1) | copy-start | bytes 3932164
  15.1 1.3 %copy-start.1 = (bf16[4,256,640]{2,1,0:T(8,128)(2,1)S(1)}, bf16[4,256,640]{2,1,0:T(8,128)(2,1)}, u32[]{:S(2)}) copy-start(bf16[4,256,640]{2,1,0:T(8,128)(2,1)} %refs_1_.1) | copy-start | bytes 3932164
  16.4 22.8 %copy-start.2 = (bf16[4,256,640]{2,1,0:T(8,128)(2,1)S(1)}, bf16[4,256,640]{2,1,0:T(8,128)(2,1)}, u32[]{:S(2)}) copy-start(bf16[4,256,640]{2,1,0:T(8,128)(2,1)} %refs_1_.1) | copy-start | bytes 3932164
  16.4 22.8 %copy-start.3 = (bf16[4,256,640]{2,1,0:T(8,128)(2,1)S(1)}, bf16[4,256,640]{2,1,0:T(8,128)(2,1)}, u32[]{:S(2)}) copy-start(bf16[4,256,640]{2,1,0:T(8,128)(2,1)} %refs_0_.1) | copy-start | bytes 3932164
  16.4 22.8 %copy-start.4 = (bf16[4,256,128]{2,1,0:T(8,128)(2,1)S(1)}, bf16[4,256,128]{2,1,0:T(8,128)(2,1)}, u32[]{:S(2)}) copy-start(bf16[4,256,128]{2,1,0:T(8,128)(2,1)} %k_ref.1) | copy-start | bytes 786436
  17.4 1.3 %collective-permute-start.3 = (f32[4,16,256]{2,1,0:T(8,128)S(1)}, f32[4,16,256]{2,1,0:T(8,128)S(1)}, u32[]{:S(2)}, u32[]{:S(2)}) collective-permute-start(f32[4,16,256]{2,1,0:T(8,128)S(1)} %stat_part.1.stat_ref.refs_2_), channel_id=1, source_target_pairs={{0,1},{1,0},{2,3},{3,2},{4,5},{5,4},{6,7},{7,6},{8,9},{9,8},{10,11... | collective-permute-start | bytes 196616 | tf_op jit(solution)/shard_map/ppermute | solution.py:340
  20.2 0.7 copy-start.6
  20.9 18.0 %collective-permute-start.6 = (bf16[4,8,16,256]{3,2,1,0:T(8,128)(2,1)}, bf16[4,8,16,256]{3,2,1,0:T(8,128)(2,1)S(1)}, u32[]{:S(2)}, u32[]{:S(2)}) collective-permute-start(bf16[4,8,16,256]{3,2,1,0:T(8,128)(2,1)} %bitcast.9), channel_id=1, source_target_pairs={{0,12},{1,21},{2,14},{3,23},{4,16},{5,25},{6,18},{7,27},{8,20},{9,... | collective-permute-start | bytes 786440 | tf_op jit(solution)/shard_map/ppermute | solution.py:347
  27.4 14.9 %collective-permute-start.5 = (bf16[4,8,16,256]{3,2,1,0:T(8,128)(2,1)}, bf16[4,8,16,256]{3,2,1,0:T(8,128)(2,1)S(1)}, u32[]{:S(2)}, u32[]{:S(2)}) collective-permute-start(bf16[4,8,16,256]{3,2,1,0:T(8,128)(2,1)} %bitcast.10), channel_id=1, source_target_pairs={{0,8},{1,25},{2,10},{3,27},{4,12},{5,29},{6,14},{7,31},{8,16},{9,1... | collective-permute-start | bytes 786440 | tf_op jit(solution)/shard_map/ppermute | solution.py:346
  27.7 17.4 %collective-permute-start.4 = (bf16[4,8,16,256]{3,2,1,0:T(8,128)(2,1)}, bf16[4,8,16,256]{3,2,1,0:T(8,128)(2,1)S(1)}, u32[]{:S(2)}, u32[]{:S(2)}) collective-permute-start(bf16[4,8,16,256]{3,2,1,0:T(8,128)(2,1)} %bitcast.11), channel_id=1, source_target_pairs={{0,4},{1,29},{2,6},{3,31},{4,8},{5,1},{6,10},{7,3},{8,12},{9,5},{1... | collective-permute-start | bytes 786440 | tf_op jit(solution)/shard_map/ppermute | solution.py:345
  39.0 2.7 %copy-start.7 = (bf16[32,16,256]{2,1,0:T(8,128)(2,1)S(1)}, bf16[32,16,256]{2,1,0:T(8,128)(2,1)}, u32[]{:S(2)}) copy-start(bf16[32,16,256]{2,1,0:T(8,128)(2,1)} %copy-done.6) | copy-start | bytes 786436
  39.0 7.4 %collective-permute-start.7 = (bf16[2,8,16,256]{3,2,1,0:T(8,128)(2,1)S(1)}, bf16[2,8,16,256]{3,2,1,0:T(8,128)(2,1)S(1)}, u32[]{:S(2)}, u32[]{:S(2)}) collective-permute-start(bf16[2,8,16,256]{3,2,1,0:T(8,128)(2,1)S(1)} %constant_dynamic-slice_fusion), channel_id=1, source_target_pairs={{0,4},{1,29},{2,6},{3,31},{4,8},{5,1},{6,10},{7,3},{8,12},{9,5},{1... | collective-permute-start | bytes 393224 | tf_op jit(solution)/shard_map/ppermute | solution.py:349
  52.0 14.8 %collective-permute-start.10 = (bf16[4,256,640]{2,1,0:T(8,128)(2,1)S(1)}, bf16[4,256,640]{2,1,0:T(8,128)(2,1)S(1)}, u32[]{:S(2)}, u32[]{:S(2)}) collective-permute-start(bf16[4,256,640]{2,1,0:T(8,128)(2,1)S(1)} %get-tuple-element.37), channel_id=1, source_target_pairs={{0,1},{1,0},{2,3},{3,2},{4,5},{5,4},{6,7},{7,6},{8,9},{9,8},{10,11... | collective-permute-start | bytes 3932168 | tf_op jit(solution)/shard_map/ppermute | solution.py:366
  53.0 6.6 %collective-permute-start.11 = (bf16[2,8,16,256]{3,2,1,0:T(8,128)(2,1)S(1)}, bf16[2,8,16,256]{3,2,1,0:T(8,128)(2,1)S(1)}, u32[]{:S(2)}, u32[]{:S(2)}) collective-permute-start(bf16[2,8,16,256]{3,2,1,0:T(8,128)(2,1)S(1)} %get-tuple-element.43), channel_id=1, source_target_pairs={{0,28},{1,5},{2,30},{3,7},{4,0},{5,9},{6,2},{7,11},{8,4},{9,13},{1... | collective-permute-start | bytes 393224 | tf_op jit(solution)/shard_map/ppermute | solution.py:361
  53.5 8.9 %collective-permute-start.8 = (bf16[4,8,16,256]{3,2,1,0:T(8,128)(2,1)S(1)}, bf16[4,8,16,256]{3,2,1,0:T(8,128)(2,1)S(1)}, u32[]{:S(2)}, u32[]{:S(2)}) collective-permute-start(bf16[4,8,16,256]{3,2,1,0:T(8,128)(2,1)S(1)} %get-tuple-element.34), channel_id=1, source_target_pairs={{0,28},{1,5},{2,30},{3,7},{4,0},{5,9},{6,2},{7,11},{8,4},{9,13},{1... | collective-permute-start | bytes 786440 | tf_op jit(solution)/shard_map/ppermute | solution.py:365
  55.0 11.7 %collective-permute-start.9 = (bf16[4,8,16,256]{3,2,1,0:T(8,128)(2,1)S(1)}, bf16[4,8,16,256]{3,2,1,0:T(8,128)(2,1)S(1)}, u32[]{:S(2)}, u32[]{:S(2)}) collective-permute-start(bf16[4,8,16,256]{3,2,1,0:T(8,128)(2,1)S(1)} %get-tuple-element.35), channel_id=1, source_target_pairs={{0,24},{1,9},{2,26},{3,11},{4,28},{5,13},{6,30},{7,15},{8,0},{9,17... | collective-permute-start | bytes 786440 | tf_op jit(solution)/shard_map/ppermute | solution.py:364
  59.8 18.8 %collective-permute-start.12 = (bf16[4,8,16,256]{3,2,1,0:T(8,128)(2,1)S(1)}, bf16[4,8,16,256]{3,2,1,0:T(8,128)(2,1)S(1)}, u32[]{:S(2)}, u32[]{:S(2)}) collective-permute-start(bf16[4,8,16,256]{3,2,1,0:T(8,128)(2,1)S(1)} %add_convert_fusion.2), channel_id=1, source_target_pairs={{0,20},{1,13},{2,22},{3,15},{4,24},{5,17},{6,26},{7,19},{8,28},{9,... | collective-permute-start | bytes 786440 | tf_op jit(solution)/shard_map/ppermute | solution.py:363

commit v3 on v2

--- a/solution.py
+++ b/solution.py
@@ -338,8 +338,8 @@
     q_oth, do_oth = swap(queries), swap(out_grad)
     stat = stat_part(attn_out, out_grad, logsumexp)
     stat_oth = swap(stat)
-    plane, prefixes, q_oth, do_oth, count, stat, stat_oth = lax.optimization_barrier(
-        (plane, prefixes, q_oth, do_oth, counts, stat, stat_oth)
+    plane, prefixes, q_oth, do_oth, count, stat = lax.optimization_barrier(
+        (plane, prefixes, q_oth, do_oth, counts, stat)
     )
     own_half = lax.dynamic_slice_in_dim(plane, core * (NY * NC // 2), NY * NC // 2, 0)
     one = lax.ppermute(plane, "br", ring_perm(1))

time: 94.9 us -> 93.4 us (0.984); the launches traced: 94.7 us -> 91.8 us
  Pallas kernels: 12.2 us -> 17.7 us
  waiting for transfers between devices: 34.1 us -> 29.6 us
  blocking collectives: 14.4 us -> 11.8 us
  starting transfers between devices: 25.9 us -> 24.3 us
    pallas_call x1, Pallas kernels: 5.6 us -> 8.65 us  [prefix_part(): pl.pallas_call(functools.partial(prefix_kernel, len(pieces), slots, len(o...]
    all_to_all x1, blocking collectives: 14.4 us -> 11.8 us  [plane_exchange(): lax.all_to_all(blocks, ('br', 'own'), split_axis=0, concat_axis=0, tiled=...]
    pallas_call x1, Pallas kernels: 2.51 us -> 4.95 us  [self_part(): pl.pallas_call(self_kernel, grid=(slots,), in_specs=[smem(), wide, narrow...]
    ppermute x1, waiting for transfers between devices: 2.81 us -> 0.57 us  [per_device(): one = lax.ppermute(plane, 'br', ring_perm(1))]
    ppermute x1, starting transfers between devices: 3.67 us -> 5.31 us  [per_device(): h2 = lax.ppermute(g2, 'br', ring_perm(-2))]
    ppermute x1, starting transfers between devices: 1.55 us -> 0.08 us  [per_device(): h1 = lax.ppermute(g1, 'br', ring_perm(-1))]
    all_to_all x1, waiting for transfers between devices: 1.48 us -> 2.71 us  [plane_exchange(): lax.all_to_all(blocks, ('br', 'own'), split_axis=0, concat_axis=0, tiled=...]
    ppermute x1, waiting for transfers between devices: 10.3 us -> 9.37 us  [per_device(): h3 = lax.ppermute((g3.astype(f32) + far).astype(bf16), 'br', ring_perm(-3))]
  transfers between devices with their start and end apart: 14 -> 14, of which waited for: 10 -> 7; matrix products, arithmetic and copies ran while one was open for 3% -> 4% of each run, Pallas kernels for 5% -> 8%
where the time goes in v3:
time: 93.4 us; the launch traced here: 91.8 us
  waiting for transfers between devices  29.6 us (32%)
  starting transfers between devices  24.3 us (26%)
  Pallas kernels  17.7 us (19%)
  blocking collectives  11.8 us (13%)
  local copies, waits for them, and re-layouts  4.3 us (5%)
  other arithmetic  2.57 us (3%)
  between operations  1.44 us (2%)
    all_to_all x1, blocking collectives, plane_exchange(): lax.all_to_all(blocks, ('br', 'own'), split_axis=0, concat_axis=0, tiled=...  11.8 us
    ppermute x1, waiting for transfers between devices, per_device(): three = lax.ppermute(plane, 'br', ring_perm(3))  10.3 us
    ppermute x1, waiting for transfers between devices, per_device(): h3 = lax.ppermute((g3.astype(f32) + far).astype(bf16), 'br', ring_perm(-3))  9.37 us
    pallas_call x1, Pallas kernels, prefix_part(): pl.pallas_call(functools.partial(prefix_kernel, len(pieces), slots, len(o...  8.65 us
    ppermute x1, starting transfers between devices, per_device(): three = lax.ppermute(plane, 'br', ring_perm(3))  6.47 us
    all_to_all x1, starting transfers between devices, plane_exchange(): lax.all_to_all(blocks, ('br', 'own'), split_axis=0, concat_axis=0, tiled=...  5.94 us
    ppermute x1, starting transfers between devices, per_device(): h2 = lax.ppermute(g2, 'br', ring_perm(-2))  5.31 us
    pallas_call x1, Pallas kernels, self_part(): pl.pallas_call(self_kernel, grid=(slots,), in_specs=[smem(), wide, narrow...  4.95 us
  transfers between devices with their start and end apart: 14, of which 7 were waited for; matrix products, arithmetic and copies ran while one was open for 4% of the time, Pallas kernels for 8%

profile of v3, /device:TPU:1, one launch (start us, length us, event | category | flops | bytes accessed | tf_op | source)
XLA Modules:
  0.0 91.8 jit_solution(8213834953271566806)
XLA Ops:
  0.6 3.3 %collective-permute-start.1 = (bf16[4,256,640]{2,1,0:T(8,128)(2,1)}, bf16[4,256,640]{2,1,0:T(8,128)(2,1)}, u32[]{:S(2)}, u32[]{:S(2)}) collective-permute-start(bf16[4,256,640]{2,1,0:T(8,128)(2,1)} %refs_0_.1), channel_id=1, source_target_pairs={{0,1},{1,0},{2,3},{3,2},{4,5},{5,4},{6,7},{7,6},{8,9},{9,8},{10,11... | collective-permute-start | bytes 3932168 | tf_op jit(solution)/shard_map/ppermute | solution.py:338
  4.0 0.1 collective-permute-start.2
  4.1 1.5 %send_part.1 = bf16[32,16,256]{2,1,0:T(8,128)(2,1)} custom-call(bf16[16,1024]{1,0:T(8,128)(2,1)} %bitcast.9, bf16[16,1024]{1,0:T(8,128)(2,1)} %bitcast.10), custom_call_target="tpu_custom_call" | custom-call | tf_op jit(solution)/shard_map/send_part/pallas_call | solution.py:103
  5.6 5.9 %all-to-all-start = ((bf16[32,16,256]{2,1,0:T(8,128)(2,1)}), bf16[32,16,256]{2,1,0:T(8,128)(2,1)}, u32[]{:S(2)}, u32[]{:S(2)}) async-start(bf16[32,16,256]{2,1,0:T(8,128)(2,1)} %send_part.1), calls=%async_computation | async-start | bytes 524288 | tf_op jit(solution)/shard_map/all_to_all | solution.py:46
  12.2 0.7 compare_select_fusion
  12.8 0.3 collective-permute-start
  13.1 0.7 copy.15.lse_ref
  13.9 1.3 %copy-done = bf16[4,256,640]{2,1,0:T(8,128)(2,1)S(1)} copy-done((bf16[4,256,640]{2,1,0:T(8,128)(2,1)S(1)}, bf16[4,256,640]{2,1,0:T(8,128)(2,1)}, u32[]{:S(2)}) %copy-start) | copy-done | bytes 1310744
  15.2 1.3 %copy-done.1 = bf16[4,256,640]{2,1,0:T(8,128)(2,1)S(1)} copy-done((bf16[4,256,640]{2,1,0:T(8,128)(2,1)S(1)}, bf16[4,256,640]{2,1,0:T(8,128)(2,1)}, u32[]{:S(2)}) %copy-start.1) | copy-done | bytes 1310744
  16.5 1.0 %stat_part.1.stat_ref.refs_2_ = f32[4,16,256]{2,1,0:T(8,128)S(1)} custom-call(bf16[4,256,640]{2,1,0:T(8,128)(2,1)S(1)} %copy-done, bf16[4,256,640]{2,1,0:T(8,128)(2,1)S(1)} %copy-done.1, f32[4,5,256]{2,1,0:T(8,128)S(1)} %copy.15.lse_ref), custom_call_target="tpu_custom_call" | custom-call | flops 1310720 | bytes 2621440 | tf_op jit(solution)/shard_map/stat_part/pallas_call | solution.py:147
  17.5 0.0 collective-permute-done
  17.6 0.1 pad_add_fusion.pre_ref
  17.6 2.7 %all-to-all-done = bf16[32,16,256]{2,1,0:T(8,128)(2,1)} async-done(((bf16[32,16,256]{2,1,0:T(8,128)(2,1)}), bf16[32,16,256]{2,1,0:T(8,128)(2,1)}, u32[]{:S(2)}, u32[]{:S(2)}) %all-to-all-start) | async-done | bytes 262176 | tf_op jit(solution)/shard_map/all_to_all | solution.py:46
  20.3 0.0 collective-permute-done.1.refs_3_
  20.3 0.0 collective-permute-done.2.refs_4_
  20.3 6.5 %collective-permute-start.6 = (bf16[4,8,16,256]{3,2,1,0:T(8,128)(2,1)}, bf16[4,8,16,256]{3,2,1,0:T(8,128)(2,1)S(1)}, u32[]{:S(2)}, u32[]{:S(2)}) collective-permute-start(bf16[4,8,16,256]{3,2,1,0:T(8,128)(2,1)} %bitcast.2), channel_id=1, source_target_pairs={{0,12},{1,21},{2,14},{3,23},{4,16},{5,25},{6,18},{7,27},{8,20},{9,... | collective-permute-start | bytes 786440 | tf_op jit(solution)/shard_map/ppermute | solution.py:347
  26.8 0.0 collective-permute-start.3
  26.8 0.3 collective-permute-start.5
  27.1 0.5 collective-permute-start.4
  27.6 10.3 %collective-permute-done.6.refs_10_ = bf16[4,8,16,256]{3,2,1,0:T(8,128)(2,1)S(1)} collective-permute-done((bf16[4,8,16,256]{3,2,1,0:T(8,128)(2,1)}, bf16[4,8,16,256]{3,2,1,0:T(8,128)(2,1)S(1)}, u32[]{:S(2)}, u32[]{:S(2)}) %collective-permute-start.6) | collective-permute-done | bytes 262176 | tf_op jit(solution)/shard_map/ppermute | solution.py:347
  37.9 0.1 collective-permute-start.7
  38.0 0.0 copy-done.5
  38.0 0.0 copy-done.2
  38.0 0.0 copy-done.3
  38.0 0.0 copy-done.4
  38.0 5.0 %self_part.1 = (bf16[4,256,640]{2,1,0:T(8,128)(2,1)S(1)}, bf16[4,256,128]{2,1,0:T(8,128)(2,1)}, bf16[4,256,128]{2,1,0:T(8,128)(2,1)}) custom-call(s32[1]{0:T(128)} %copy.16.count_ref, bf16[4,256,640]{2,1,0:T(8,128)(2,1)S(1)} %copy-done.3, bf16[4,256,128]{2,1,0:T(8,128)(2,1)S(1)} %copy-done.4, bf16[4,256,128]{2,1,0:T(8,128)(2,1)S(1)} %copy-done.5, ...), custom_call_target="tpu_custom_call" | custom-call | flops 1677721600 | bytes 6553600 | tf_op jit(solution)/shard_map/self_part/pallas_call | solution.py:195
  43.0 0.9 constant_dynamic-slice_fusion.1.refs_7_
  43.9 0.0 collective-permute-done.3.refs_5_
  43.9 0.0 collective-permute-done.5.refs_9_
  43.9 0.6 collective-permute-done.4.refs_8_
  44.5 1.3 %collective-permute-done.7.refs_11_ = bf16[2,8,16,256]{3,2,1,0:T(8,128)(2,1)S(1)} collective-permute-done((bf16[2,8,16,256]{3,2,1,0:T(8,128)(2,1)S(1)}, bf16[2,8,16,256]{3,2,1,0:T(8,128)(2,1)S(1)}, u32[]{:S(2)}, u32[]{:S(2)}) %collective-permute-start.7) | collective-permute-done | bytes 131104 | tf_op jit(solution)/shard_map/ppermute | solution.py:349
  45.8 8.7 %prefix_part.1 = (bf16[4,256,640]{2,1,0:T(8,128)(2,1)S(1)}, bf16[4,256,640]{2,1,0:T(8,128)(2,1)S(1)}, bf16[2,8,16,256]{3,2,1,0:T(8,128)(2,1)S(1)}, bf16[4,8,16,2...) custom-call(s32[8]{0:T(128)S(1)} %pad_add_fusion.pre_ref, ...), custom_call_target="tpu_custom_call" | custom-call | flops 3355443200 | bytes 10485760 | tf_op jit(solution)/shard_map/prefix_part/pallas_call | solution.py:291
  54.4 0.1 collective-permute-start.10
  54.5 0.1 collective-permute-start.11
  54.6 0.1 collective-permute-start.8
  54.7 5.3 %collective-permute-start.9 = (bf16[4,8,16,256]{3,2,1,0:T(8,128)(2,1)S(1)}, bf16[4,8,16,256]{3,2,1,0:T(8,128)(2,1)S(1)}, u32[]{:S(2)}, u32[]{:S(2)}) collective-permute-start(bf16[4,8,16,256]{3,2,1,0:T(8,128)(2,1)S(1)} %get-tuple-element.33), channel_id=1, source_target_pairs={{0,24},{1,9},{2,26},{3,11},{4,28},{5,13},{6,30},{7,15},{8,0},{9,17... | collective-permute-start | bytes 786440 | tf_op jit(solution)/shard_map/ppermute | solution.py:364
  60.1 0.0 collective-permute-done.11
  60.1 0.2 add_convert_fusion.2
  60.2 1.7 %collective-permute-start.12 = (bf16[4,8,16,256]{3,2,1,0:T(8,128)(2,1)S(1)}, bf16[4,8,16,256]{3,2,1,0:T(8,128)(2,1)S(1)}, u32[]{:S(2)}, u32[]{:S(2)}) collective-permute-start(bf16[4,8,16,256]{3,2,1,0:T(8,128)(2,1)S(1)} %add_convert_fusion.2), channel_id=1, source_target_pairs={{0,20},{1,13},{2,22},{3,15},{4,24},{5,17},{6,26},{7,19},{8,28},{9,... | collective-permute-start | bytes 786440 | tf_op jit(solution)/shard_map/ppermute | solution.py:363
  62.0 0.5 collective-permute-done.8
  62.5 4.9 %collective-permute-done.9 = bf16[4,8,16,256]{3,2,1,0:T(8,128)(2,1)S(1)} collective-permute-done((bf16[4,8,16,256]{3,2,1,0:T(8,128)(2,1)S(1)}, bf16[4,8,16,256]{3,2,1,0:T(8,128)(2,1)S(1)}, u32[]{:S(2)}, u32[]{:S(2)}) %collective-permute-start.9) | collective-permute-done | bytes 262176 | tf_op jit(solution)/shard_map/ppermute | solution.py:364
  67.3 0.1 convert_add_fusion
  67.4 0.0 collective-permute-done.10
  67.4 1.4 %add_convert_fusion = bf16[4,256,640]{2,1,0:T(8,128)(2,1)} fusion(bf16[4,256,640]{2,1,0:T(8,128)(2,1)S(1)} %collective-permute-done.10, bf16[4,256,640]{2,1,0:T(8,128)(2,1)S(1)} %get-tuple-element.34), kind=kLoop, calls=%fused_computation | loop fusion | flops 2621440 | bytes 3932160 | tf_op jit(solution)/shard_map/convert_element_type | solution.py:367
  68.8 9.4 %collective-permute-done.12 = bf16[4,8,16,256]{3,2,1,0:T(8,128)(2,1)S(1)} collective-permute-done((bf16[4,8,16,256]{3,2,1,0:T(8,128)(2,1)S(1)}, bf16[4,8,16,256]{3,2,1,0:T(8,128)(2,1)S(1)}, u32[]{:S(2)}, u32[]{:S(2)}) %collective-permute-start.12) | collective-permute-done | bytes 262176 | tf_op jit(solution)/shard_map/ppermute | solution.py:363
  78.2 0.2 add_convert_fusion.1
  78.4 11.8 %all_to_all.10.in_ref = bf16[32,16,256]{2,1,0:T(8,128)(2,1)} all-to-all(bf16[32,16,256]{2,1,0:T(8,128)(2,1)S(1)} %bitcast.8), channel_id=1, replica_groups={{0,32,64,96,128,160,192,224,1,33,65,97,129,161,193,225,2,34,66,98,130,1..., dimensions={0} | all-to-all | bytes 524288 | tf_op jit(solution)/shard_map/all_to_all | solution.py:46
  90.2 1.6 %home_part.1 = (bf16[16,1024]{1,0:T(8,128)(2,1)}, bf16[16,1024]{1,0:T(8,128)(2,1)}) custom-call(bf16[32,16,256]{2,1,0:T(8,128)(2,1)} %all_to_all.10.in_ref), custom_call_target="tpu_custom_call" | custom-call | tf_op jit(solution)/shard_map/home_part/pallas_call | solution.py:124
  (8 shorter events, 0.0 us)
Async XLA Ops:
  0.6 19.7 %collective-permute-start.1 = (bf16[4,256,640]{2,1,0:T(8,128)(2,1)}, bf16[4,256,640]{2,1,0:T(8,128)(2,1)}, u32[]{:S(2)}, u32[]{:S(2)}) collective-permute-start(bf16[4,256,640]{2,1,0:T(8,128)(2,1)} %refs_0_.1), channel_id=1, source_target_pairs={{0,1},{1,0},{2,3},{3,2},{4,5},{5,4},{6,7},{7,6},{8,9},{9,8},{10,11... | collective-permute-start | bytes 3932168 | tf_op jit(solution)/shard_map/ppermute | solution.py:338
  4.0 16.4 %collective-permute-start.2 = (bf16[4,256,640]{2,1,0:T(8,128)(2,1)}, bf16[4,256,640]{2,1,0:T(8,128)(2,1)}, u32[]{:S(2)}, u32[]{:S(2)}) collective-permute-start(bf16[4,256,640]{2,1,0:T(8,128)(2,1)} %refs_1_.1), channel_id=1, source_target_pairs={{0,1},{1,0},{2,3},{3,2},{4,5},{5,4},{6,7},{7,6},{8,9},{9,8},{10,11... | collective-permute-start | bytes 3932168 | tf_op jit(solution)/shard_map/ppermute | solution.py:338
  5.6 32.4 %copy-start.5 = (bf16[4,256,128]{2,1,0:T(8,128)(2,1)S(1)}, bf16[4,256,128]{2,1,0:T(8,128)(2,1)}, u32[]{:S(2)}) copy-start(bf16[4,256,128]{2,1,0:T(8,128)(2,1)} %v_ref.1) | copy-start | bytes 786436
  5.6 14.8 %all-to-all-start = ((bf16[32,16,256]{2,1,0:T(8,128)(2,1)}), bf16[32,16,256]{2,1,0:T(8,128)(2,1)}, u32[]{:S(2)}, u32[]{:S(2)}) async-start(bf16[32,16,256]{2,1,0:T(8,128)(2,1)} %send_part.1), calls=%async_computation | async-start | bytes 524288 | tf_op jit(solution)/shard_map/all_to_all | solution.py:46
  12.8 4.7 %collective-permute-start = (s32[4]{0:T(128)S(1)}, s32[4]{0:T(128)S(1)}, u32[]{:S(2)}, u32[]{:S(2)}) collective-permute-start(s32[4]{0:T(128)S(1)} %compare_select_fusion), channel_id=1, source_target_pairs={{0,1},{1,0},{2,3},{3,2},{4,5},{5,4},{6,7},{7,6},{8,9},{9,8},{10,11... | collective-permute-start | bytes 56 | tf_op jit(solution)/shard_map/ppermute | solution.py:337
  13.9 1.3 %copy-start = (bf16[4,256,640]{2,1,0:T(8,128)(2,1)S(1)}, bf16[4,256,640]{2,1,0:T(8,128)(2,1)}, u32[]{:S(2)}) copy-start(bf16[4,256,640]{2,1,0:T(8,128)(2,1)} %o_ref.1) | copy-start | bytes 3932164
  15.2 1.3 %copy-start.1 = (bf16[4,256,640]{2,1,0:T(8,128)(2,1)S(1)}, bf16[4,256,640]{2,1,0:T(8,128)(2,1)}, u32[]{:S(2)}) copy-start(bf16[4,256,640]{2,1,0:T(8,128)(2,1)} %refs_1_.1) | copy-start | bytes 3932164
  16.5 21.5 %copy-start.2 = (bf16[4,256,640]{2,1,0:T(8,128)(2,1)S(1)}, bf16[4,256,640]{2,1,0:T(8,128)(2,1)}, u32[]{:S(2)}) copy-start(bf16[4,256,640]{2,1,0:T(8,128)(2,1)} %refs_1_.1) | copy-start | bytes 3932164
  16.5 21.5 %copy-start.3 = (bf16[4,256,640]{2,1,0:T(8,128)(2,1)S(1)}, bf16[4,256,640]{2,1,0:T(8,128)(2,1)}, u32[]{:S(2)}) copy-start(bf16[4,256,640]{2,1,0:T(8,128)(2,1)} %refs_0_.1) | copy-start | bytes 3932164
  16.5 21.5 %copy-start.4 = (bf16[4,256,128]{2,1,0:T(8,128)(2,1)S(1)}, bf16[4,256,128]{2,1,0:T(8,128)(2,1)}, u32[]{:S(2)}) copy-start(bf16[4,256,128]{2,1,0:T(8,128)(2,1)} %k_ref.1) | copy-start | bytes 786436
  20.3 17.5 %collective-permute-start.6 = (bf16[4,8,16,256]{3,2,1,0:T(8,128)(2,1)}, bf16[4,8,16,256]{3,2,1,0:T(8,128)(2,1)S(1)}, u32[]{:S(2)}, u32[]{:S(2)}) collective-permute-start(bf16[4,8,16,256]{3,2,1,0:T(8,128)(2,1)} %bitcast.2), channel_id=1, source_target_pairs={{0,12},{1,21},{2,14},{3,23},{4,16},{5,25},{6,18},{7,27},{8,20},{9,... | collective-permute-start | bytes 786440 | tf_op jit(solution)/shard_map/ppermute | solution.py:347
  26.8 17.1 %collective-permute-start.3 = (f32[4,16,256]{2,1,0:T(8,128)S(1)}, f32[4,16,256]{2,1,0:T(8,128)S(1)}, u32[]{:S(2)}, u32[]{:S(2)}) collective-permute-start(f32[4,16,256]{2,1,0:T(8,128)S(1)} %stat_part.1.stat_ref.refs_2_), channel_id=1, source_target_pairs={{0,1},{1,0},{2,3},{3,2},{4,5},{5,4},{6,7},{7,6},{8,9},{9,8},{10,11... | collective-permute-start | bytes 196616 | tf_op jit(solution)/shard_map/ppermute | solution.py:340
  26.8 17.1 %collective-permute-start.5 = (bf16[4,8,16,256]{3,2,1,0:T(8,128)(2,1)}, bf16[4,8,16,256]{3,2,1,0:T(8,128)(2,1)S(1)}, u32[]{:S(2)}, u32[]{:S(2)}) collective-permute-start(bf16[4,8,16,256]{3,2,1,0:T(8,128)(2,1)} %bitcast.2), channel_id=1, source_target_pairs={{0,8},{1,25},{2,10},{3,27},{4,12},{5,29},{6,14},{7,31},{8,16},{9,1... | collective-permute-start | bytes 786440 | tf_op jit(solution)/shard_map/ppermute | solution.py:346
  27.1 17.4 %collective-permute-start.4 = (bf16[4,8,16,256]{3,2,1,0:T(8,128)(2,1)}, bf16[4,8,16,256]{3,2,1,0:T(8,128)(2,1)S(1)}, u32[]{:S(2)}, u32[]{:S(2)}) collective-permute-start(bf16[4,8,16,256]{3,2,1,0:T(8,128)(2,1)} %bitcast.2), channel_id=1, source_target_pairs={{0,4},{1,29},{2,6},{3,31},{4,8},{5,1},{6,10},{7,3},{8,12},{9,5},{1... | collective-permute-start | bytes 786440 | tf_op jit(solution)/shard_map/ppermute | solution.py:345
  37.9 7.9 %collective-permute-start.7 = (bf16[2,8,16,256]{3,2,1,0:T(8,128)(2,1)S(1)}, bf16[2,8,16,256]{3,2,1,0:T(8,128)(2,1)S(1)}, u32[]{:S(2)}, u32[]{:S(2)}) collective-permute-start(bf16[2,8,16,256]{3,2,1,0:T(8,128)(2,1)S(1)} %constant_dynamic-slice_fusion), channel_id=1, source_target_pairs={{0,4},{1,29},{2,6},{3,31},{4,8},{5,1},{6,10},{7,3},{8,12},{9,5},{1... | collective-permute-start | bytes 393224 | tf_op jit(solution)/shard_map/ppermute | solution.py:349
  54.4 13.0 %collective-permute-start.10 = (bf16[4,256,640]{2,1,0:T(8,128)(2,1)S(1)}, bf16[4,256,640]{2,1,0:T(8,128)(2,1)S(1)}, u32[]{:S(2)}, u32[]{:S(2)}) collective-permute-start(bf16[4,256,640]{2,1,0:T(8,128)(2,1)S(1)} %get-tuple-element.35), channel_id=1, source_target_pairs={{0,1},{1,0},{2,3},{3,2},{4,5},{5,4},{6,7},{7,6},{8,9},{9,8},{10,11... | collective-permute-start | bytes 3932168 | tf_op jit(solution)/shard_map/ppermute | solution.py:366
  54.5 5.5 %collective-permute-start.11 = (bf16[2,8,16,256]{3,2,1,0:T(8,128)(2,1)S(1)}, bf16[2,8,16,256]{3,2,1,0:T(8,128)(2,1)S(1)}, u32[]{:S(2)}, u32[]{:S(2)}) collective-permute-start(bf16[2,8,16,256]{3,2,1,0:T(8,128)(2,1)S(1)} %get-tuple-element.41), channel_id=1, source_target_pairs={{0,28},{1,5},{2,30},{3,7},{4,0},{5,9},{6,2},{7,11},{8,4},{9,13},{1... | collective-permute-start | bytes 393224 | tf_op jit(solution)/shard_map/ppermute | solution.py:361
  54.6 7.8 %collective-permute-start.8 = (bf16[4,8,16,256]{3,2,1,0:T(8,128)(2,1)S(1)}, bf16[4,8,16,256]{3,2,1,0:T(8,128)(2,1)S(1)}, u32[]{:S(2)}, u32[]{:S(2)}) collective-permute-start(bf16[4,8,16,256]{3,2,1,0:T(8,128)(2,1)S(1)} %get-tuple-element.32), channel_id=1, source_target_pairs={{0,28},{1,5},{2,30},{3,7},{4,0},{5,9},{6,2},{7,11},{8,4},{9,13},{1... | collective-permute-start | bytes 786440 | tf_op jit(solution)/shard_map/ppermute | solution.py:365
  54.7 12.6 %collective-permute-start.9 = (bf16[4,8,16,256]{3,2,1,0:T(8,128)(2,1)S(1)}, bf16[4,8,16,256]{3,2,1,0:T(8,128)(2,1)S(1)}, u32[]{:S(2)}, u32[]{:S(2)}) collective-permute-start(bf16[4,8,16,256]{3,2,1,0:T(8,128)(2,1)S(1)} %get-tuple-element.33), channel_id=1, source_target_pairs={{0,24},{1,9},{2,26},{3,11},{4,28},{5,13},{6,30},{7,15},{8,0},{9,17... | collective-permute-start | bytes 786440 | tf_op jit(solution)/shard_map/ppermute | solution.py:364
  60.2 17.9 %collective-permute-start.12 = (bf16[4,8,16,256]{3,2,1,0:T(8,128)(2,1)S(1)}, bf16[4,8,16,256]{3,2,1,0:T(8,128)(2,1)S(1)}, u32[]{:S(2)}, u32[]{:S(2)}) collective-permute-start(bf16[4,8,16,256]{3,2,1,0:T(8,128)(2,1)S(1)} %add_convert_fusion.2), channel_id=1, source_target_pairs={{0,20},{1,13},{2,22},{3,15},{4,24},{5,17},{6,26},{7,19},{8,28},{9,... | collective-permute-start | bytes 786440 | tf_op jit(solution)/shard_map/ppermute | solution.py:363
